TPU v7x, 768 devices: a whole 4x8x12 slice. The times are simulated.
768 devices in a mesh: dp: 96 (over y_hi, z, core), outer: 8 (over x, y_lo).
Axes of the slice: x: 4, y: 8 (y_hi: 4, y_lo: 2; y = y_hi * 2 + y_lo), z: 12, core: 2. Of those that a mesh axis runs over, the one named last changes fastest.
Arguments:
- grads: bfloat16 [8, 96, 192, 4096], P('outer', 'dp'), may hold values from -20 to 20
- momentum: float32 [8, 192, 4096], P('outer', 'dp'), may hold values from -6 to 6
- corner: int32 [192, 2], P('dp'), may hold values from 0 to 8
Outputs:
- new_momentum: float32 [8, 192, 4096], P('outer', 'dp')
- update: float32 [192, 4096], P('dp')
All inputs are finite; a program needn't handle non-finite values.
Results may differ from a plain program's by a relative error of at most 0.0003.
Values sent between devices are 32-bit elements; how exact they have to be, the bound alone decides.
No kernel may reach another device: no remote copies, remote signals or barrier semaphores. Data moves between devices by JAX's collectives and lax.ppermute only.
A program may use at most 32 MiB of HBM per device.

v0:
```python
import math

import jax
import jax.numpy as jnp
from jax import lax
from jax.sharding import PartitionSpec as P

SPAN = 64
CORNER = 8


def cosine_table(length):
    freq = jnp.arange(length, dtype=jnp.float32)[:, None]
    place = jnp.arange(length, dtype=jnp.float32)[None, :]
    factor = jnp.where(freq == 0, math.sqrt(1.0 / length), math.sqrt(2.0 / length))
    return factor * jnp.cos(math.pi * (2.0 * place + 1.0) * freq / (2.0 * length))


def pickers(corner, side, kept_side):
    across = jnp.arange(side, dtype=jnp.int32)[None, None, :]
    inside = jnp.arange(kept_side, dtype=jnp.int32)[None, :, None]
    row_pick = (across == corner[:, 0][:, None, None] + inside).astype(jnp.float32)
    col_pick = (across == corner[:, 1][:, None, None] + inside).astype(jnp.float32)
    return (row_pick, col_pick)


def forward_corner(blocks, table, row_pick, col_pick, side):
    high = lax.Precision.HIGHEST
    square = blocks.reshape(blocks.shape[0], side, side)
    coeffs = jnp.einsum("ij,kjl,ml->kim", table, square, table, precision=high)
    left = jnp.einsum("kaj,kjl->kal", row_pick, coeffs, precision=high)
    return jnp.einsum("kal,kbl->kab", left, col_pick, precision=high)


def inverse_corner(kept, table, row_pick, col_pick, side):
    high = lax.Precision.HIGHEST
    placed = jnp.einsum("kaj,kab,kbl->kjl", row_pick, kept, col_pick, precision=high)
    square = jnp.einsum("ji,kjl,lm->kim", table, placed, table, precision=high)
    return square.reshape(kept.shape[0], side * side)


def on_device(grads, momentum, corner):
    side = SPAN
    kept_side = CORNER
    local_grad = grads[0, 0]
    summed = lax.psum_scatter(local_grad.astype(jnp.float32), "dp", scatter_dimension=0, tiled=True)
    mean_grad = summed / lax.axis_size("dp")
    moment = 0.9 * momentum[0] + mean_grad
    table = cosine_table(side)
    row_pick, col_pick = pickers(corner, side, kept_side)
    kept = forward_corner(moment, table, row_pick, col_pick, side)
    new_momentum = moment - inverse_corner(kept, table, row_pick, col_pick, side)
    total = lax.psum(kept, "outer")
    average = total / lax.axis_size("outer")
    update = inverse_corner(average, table, row_pick, col_pick, side)
    return (new_momentum[None], update)


def solution(mesh):
    in_specs = (P("outer", "dp", None, None), P("outer", "dp", None), P("dp", None))
    out_specs = (P("outer", "dp", None), P("dp", None))
    return jax.shard_map(
        on_device, mesh=mesh, in_specs=in_specs, out_specs=out_specs, check_vma=False
    )
```

profile of v0, /device:TPU:8, one launch (start us, length us, event | category | flops | bytes accessed | tf_op | source)
XLA Modules:
  0.0 888.6 jit_solution(5940640853563389549)
XLA Ops:
  7.2 0.0 copy-start.1
  7.2 0.0 copy-start
  7.2 0.0 all-reduce.3.cloned.1.call-start
  7.2 3.5 bitcast_convert_fusion
  10.7 0.0 all-reduce.3.cloned.1.call-update
  10.7 1.3 dynamic-slice
  12.7 0.0 copy-done.1
  12.7 0.2 slice_reduce_fusion
  12.9 0.1 iota_add_fusion
  12.9 845.1 %all-reduce.3.cloned.1.call-done = f32[192,4096]{1,0:T(8,128)} async-done(((f32[192,4096]{1,0:T(8,128)}), f32[192,4096]{1,0:T(8,128)}) %all-reduce.3.cloned.1.call-update) | async-done | bytes 3145744
  858.1 0.0 copy-done
  858.1 0.9 fusion
  859.0 0.1 reshape.87
  859.1 0.3 fusion.11
  859.5 0.3 fusion.9
  859.8 0.2 fusion.37
  860.0 0.2 fusion.35
  860.2 0.2 fusion.36
  860.4 17.7 %psum.7 = f32[2,8,8]{2,1,0:T(8,128)S(1)} all-reduce(f32[2,8,8]{2,1,0:T(8,128)S(1)} %fusion.35), channel_id=1, replica_groups=mesh['dp'=96,'outer'=8] {'outer'}, use_global_device_ids=true, to_apply=%region_1.2 | all-reduce | flops 128 | bytes 1024 | tf_op jit(solution)/shard_map/psum | solution.py:53
  878.1 0.2 fusion.34
  878.4 0.4 fusion.7
  878.8 0.3 fusion.5
  879.1 0.1 reshape.88
  879.2 0.6 subtract_bitcast_fusion
  879.8 0.2 fusion.31
  880.0 0.3 fusion.33
  880.3 0.4 fusion.3
  880.7 0.3 fusion.1
  881.0 0.7 reshape.89
  (1 shorter events, 0.0 us)
Async XLA Ops:
  7.2 5.5 copy-start.1
  7.2 850.9 %copy-start = (f32[1,2,4096]{2,1,0:T(2,128)S(1)}, f32[1,2,4096]{2,1,0:T(2,128)}, u32[]{:S(2)}) copy-start(f32[1,2,4096]{2,1,0:T(2,128)} %param.4) | copy-start | bytes 98308
  7.2 850.9 %all-reduce.3.cloned.1.call-start = ((), (), s32[]{:S(2)}) async-start(), calls=%async_computation | async-start | bytes 6291456
Sparse Core Ops, SparseCore 0:
  11.2 846.7 all-reduce.2
where the time goes:
time: 889 us
  waiting for transfers between devices  845 us (95%)
  blocking collectives  17.7 us (2%)
  between operations  14.8 us (2%)
    unnamed x2, waiting for transfers between devices  845 us
  transfers between devices with their start and end apart: 1, of which 1 were waited for; matrix products, arithmetic and copies ran while one was open for 0% of the time, Pallas kernels for 0%

commit v1 on v0

v1 whole, which is shorter than its diff:
```python
import math

import jax
import jax.numpy as jnp
import numpy as np
from jax import lax
from jax.experimental import pallas as pl
from jax.experimental.pallas import tpu as pltpu
from jax.sharding import PartitionSpec as P

SPAN = 64
CORNER = 8
LOW = 16
NY, NZ = 4, 12
N_DP = 96
N_OUTER = 8
HIGH = lax.Precision.HIGHEST


def device_of(y, z, core):
    return ((y % NY) * NZ + z % NZ) * 2 + core


def shift(dz=0, dcore=0):
    return [
        (device_of(y, z, c), device_of(y, z + dz, c ^ dcore))
        for y in range(NY)
        for z in range(NZ)
        for c in range(2)
    ]


def far_groups():
    return [
        [device_of(y, 3 * q + s, c) for q in range(4) for y in range(NY)]
        for s in range(3)
        for c in range(2)
    ]


def tables():
    k = np.arange(SPAN)[:, None]
    n = np.arange(SPAN)[None, :]
    scale = np.where(k == 0, math.sqrt(1.0 / SPAN), math.sqrt(2.0 / SPAN))
    full = scale * np.cos(np.pi * (2 * n + 1) * k / (2.0 * SPAN))
    low = full[:LOW]
    left = np.zeros((2, 2, LOW, 2, 32))
    for h in range(2):
        for b in range(2):
            left[h, b, :, b, :] = low[:, h::2]
    left = left.reshape(64, 64)
    right = np.zeros((128, 128))
    right[:, :LOW] = np.concatenate([low.T, low.T], axis=0)
    return tuple(np.asarray(v, np.float32) for v in (left, left.T, right, right.T))


def arrange_kernel(grads, send, own, square):
    place = lax.axis_index("dp")
    core = lax.rem(place, 2)
    z = lax.rem(place // 2, NZ)

    def spread(i, carry):
        rows = pl.multiple_of(i * 16, 16)
        for t in range(32):
            tile = grads[0, 0, pl.ds(rows, 16), t * 128 : (t + 1) * 128].astype(jnp.float32)
            square[pl.ds(rows * 32 + t, 16, stride=32), :] = tile
        return carry

    lax.fori_loop(0, 12, spread, 0)
    kinds = [lax.rem(z + d, 3) for d in (1, 2, 0)]

    def deal(i, carry):
        q, y = i // NY, lax.rem(i, NY)
        for slot, kind in enumerate(kinds):
            chip = y * NZ + 3 * q + kind
            for ref, c in ((send, 1 - core), (own, core)):
                first = pl.multiple_of((chip * 2 + c) * 64, 64)
                ref[slot, i] = square[pl.ds(first, 64), :]
        return carry

    lax.fori_loop(0, 16, deal, 0)


def arrange(grads):
    shape = jax.ShapeDtypeStruct((3, 16, 64, 128), jnp.float32)
    vmem = pl.BlockSpec(memory_space=pltpu.VMEM)
    return pl.pallas_call(
        arrange_kernel,
        out_shape=(shape, shape),
        in_specs=[vmem],
        out_specs=(vmem, vmem),
        scratch_shapes=[pltpu.VMEM((6144, 128), jnp.float32)],
        compiler_params=pltpu.CompilerParams(vmem_limit_bytes=24 << 20),
    )(grads)


def dot(a, b):
    return jnp.dot(a, b, precision=HIGH, preferred_element_type=jnp.float32)


def same_half():
    row = lax.broadcasted_iota(jnp.int32, (64, 128), 0)
    lane = lax.broadcasted_iota(jnp.int32, (64, 128), 1)
    return (row < 32) == (lane < 64)


def rebuild(low, left_t, right_t):
    wide = dot(low, right_t)
    both = jnp.where(same_half(), jnp.concatenate([wide, wide], axis=0), 0.0)
    return dot(left_t, both)


def kept_kernel(parts, momentum, corner, left, right, moment, packed, square):
    for t in range(32):
        square[pl.ds(t, 2, stride=32), :] = momentum[0, :, t * 128 : (t + 1) * 128]
    total = parts[0]
    for k in range(1, 16):
        total = total + parts[k]
    value = 0.9 * square[...] + total / N_DP
    moment[...] = value
    half = jnp.where(same_half(), dot(left[...], value), 0.0)
    mixed = dot(half, right[...])
    low = mixed[:32] + mixed[32:]
    row = lax.broadcasted_iota(jnp.int32, (32, 128), 0)
    lane = lax.broadcasted_iota(jnp.int32, (32, 128), 1)
    first = row < LOW
    place = jnp.where(first, row, row - LOW)
    above = place - jnp.where(first, corner[0, 0], corner[1, 0])
    beside = lane - jnp.where(first, corner[0, 1], corner[1, 1])
    inside = (above >= 0) & (above < CORNER) & (beside >= 0) & (beside < CORNER)
    kept = jnp.where(inside, low, 0.0)
    pack = kept[0:8]
    for g in range(1, 4):
        pack = pack + pltpu.roll(kept[8 * g : 8 * g + 8], 16 * g, axis=1)
    for p in range(N_OUTER):
        packed[p] = pack


def unpack(pack):
    lane = lax.broadcasted_iota(jnp.int32, (8, 128), 1)
    parts = [pack] + [pltpu.roll(pack, 128 - 16 * g, axis=1) for g in range(1, 4)]
    return jnp.concatenate([jnp.where(lane < LOW, v, 0.0) for v in parts], axis=0)


def momentum_kernel(moment, packed, left_t, right_t, out, square):
    square[...] = moment[...] - rebuild(unpack(packed[0]), left_t[...], right_t[...])
    for t in range(32):
        out[0, :, t * 128 : (t + 1) * 128] = square[pl.ds(t, 2, stride=32), :]


def update_kernel(packed, left_t, right_t, out, square):
    total = packed[0]
    for p in range(1, N_OUTER):
        total = total + packed[p]
    square[...] = rebuild(unpack(total / N_OUTER), left_t[...], right_t[...])
    for t in range(32):
        out[:, t * 128 : (t + 1) * 128] = square[pl.ds(t, 2, stride=32), :]


def on_device(grads, momentum, corner):
    left, left_t, right, right_t = (jnp.asarray(v) for v in tables())
    vmem = pl.BlockSpec(memory_space=pltpu.VMEM)
    smem = pl.BlockSpec(memory_space=pltpu.SMEM)
    square = pltpu.VMEM((64, 128), jnp.float32)

    send, own = arrange(grads)
    chip = own + lax.ppermute(send, "dp", shift(dcore=1))
    from_below = lax.ppermute(chip[0], "dp", shift(dz=1))
    from_above = lax.ppermute(chip[1], "dp", shift(dz=-1))
    near = chip[2] + from_below + from_above
    parts = lax.all_to_all(near, "dp", 0, 0, axis_index_groups=far_groups(), tiled=True)

    moment, packed = pl.pallas_call(
        kept_kernel,
        out_shape=(
            jax.ShapeDtypeStruct((64, 128), jnp.float32),
            jax.ShapeDtypeStruct((N_OUTER, 8, 128), jnp.float32),
        ),
        in_specs=[vmem, vmem, smem, vmem, vmem],
        out_specs=(vmem, vmem),
        scratch_shapes=[square],
    )(parts, momentum, corner, left, right)
    shared = lax.all_to_all(packed, "outer", 0, 0, tiled=True)
    new_momentum = pl.pallas_call(
        momentum_kernel,
        out_shape=jax.ShapeDtypeStruct((1, 2, 4096), jnp.float32),
        in_specs=[vmem] * 4,
        out_specs=vmem,
        scratch_shapes=[square],
    )(moment, packed, left_t, right_t)
    update = pl.pallas_call(
        update_kernel,
        out_shape=jax.ShapeDtypeStruct((2, 4096), jnp.float32),
        in_specs=[vmem] * 3,
        out_specs=vmem,
        scratch_shapes=[square],
    )(shared, left_t, right_t)
    return (new_momentum, update)


def solution(mesh):
    in_specs = (P("outer", "dp", None, None), P("outer", "dp", None), P("dp", None))
    out_specs = (P("outer", "dp", None), P("dp", None))
    return jax.shard_map(
        on_device, mesh=mesh, in_specs=in_specs, out_specs=out_specs, check_vma=False
    )
```

time: 889 us -> 91 us (0.10)
  the two profiles are of different devices: /device:TPU:8 before, /device:TPU:64 now
where the time goes in v1:
time: 91 us; the launch traced here: 90.6 us
  blocking collectives  40.1 us (44%)
  starting transfers between devices  19.2 us (21%)
  waiting for transfers between devices  19.1 us (21%)
  Pallas kernels  8.98 us (10%)
  local copies, waits for them, and re-layouts  2.11 us (2%)
    all_to_all x1, blocking collectives, on_device(): lax.all_to_all(near, 'dp', 0, 0, axis_index_groups=far_groups(), tiled=True)  40.1 us
    ppermute x1, waiting for transfers between devices, on_device(): from_below = lax.ppermute(chip[0], 'dp', shift(dz=1))  10.3 us
    ppermute x1, starting transfers between devices, on_device(): from_above = lax.ppermute(chip[1], 'dp', shift(dz=-1))  8.21 us
    all_to_all x1, starting transfers between devices, on_device(): shared = lax.all_to_all(packed, 'outer', 0, 0, tiled=True)  4.79 us
    all_to_all x1, waiting for transfers between devices, on_device(): shared = lax.all_to_all(packed, 'outer', 0, 0, tiled=True)  4.29 us
    ppermute x1, starting transfers between devices, on_device(): from_below = lax.ppermute(chip[0], 'dp', shift(dz=1))  4.28 us
    ppermute x1, waiting for transfers between devices, on_device(): chip = own + lax.ppermute(send, 'dp', shift(dcore=1))  3.38 us
    pallas_call x1, Pallas kernels, arrange(): pl.pallas_call(arrange_kernel, out_shape=(shape, shape), in_specs=[vmem],...  2.88 us
  transfers between devices with their start and end apart: 4, of which 4 were waited for; matrix products, arithmetic and copies ran while one was open for 0% of the time, Pallas kernels for 2%

profile of v1, /device:TPU:64, one launch (start us, length us, event | category | flops | bytes accessed | tf_op | source)
XLA Modules:
  0.0 90.6 jit_solution(10700785646052999937)
XLA Ops:
  0.6 0.0 copy-start
  0.6 1.4 %copy-done = bf16[1,1,192,4096]{3,2,1,0:T(8,128)(2,1)S(1)} copy-done((bf16[1,1,192,4096]{3,2,1,0:T(8,128)(2,1)S(1)}, bf16[1,1,192,4096]{3,2,1,0:T(8,128)(2,1)}, u32[]{:S(2)}) %copy-start) | copy-done | bytes 1572888
  2.0 2.9 %shard_map.86 = (f32[3,16,64,128]{3,2,1,0:T(8,128)S(1)}, f32[3,16,64,128]{3,2,1,0:T(8,128)S(1)}) custom-call(bf16[1,1,192,4096]{3,2,1,0:T(8,128)(2,1)S(1)} %copy-done), custom_call_target="tpu_custom_call" | custom-call | tf_op jit(solution)/shard_map/pallas_call | solution.py:87
  4.9 1.9 %collective-permute-start = (f32[3,16,64,128]{3,2,1,0:T(8,128)S(1)}, f32[3,16,64,128]{3,2,1,0:T(8,128)S(1)}, u32[]{:S(2)}, u32[]{:S(2)}) collective-permute-start(f32[3,16,64,128]{3,2,1,0:T(8,128)S(1)} %get-tuple-element.7), channel_id=1, source_target_pairs={{0,8},{8,0},{16,24},{24,16},{32,40},{40,32},{48,56},{56,48},{64,72... | collective-permute-start | bytes 4718600 | tf_op jit(solution)/shard_map/ppermute | solution.py:167
  6.9 3.4 %collective-permute-done = f32[3,16,64,128]{3,2,1,0:T(8,128)S(1)} collective-permute-done((f32[3,16,64,128]{3,2,1,0:T(8,128)S(1)}, f32[3,16,64,128]{3,2,1,0:T(8,128)S(1)}, u32[]{:S(2)}, u32[]{:S(2)}) %collective-permute-start) | collective-permute-done | bytes 1572896 | tf_op jit(solution)/shard_map/ppermute | solution.py:167
  10.2 0.3 add.9
  10.5 0.1 slice_bitcast_fusion.1
  10.6 4.3 %collective-permute-start.1 = (f32[16,64,128]{2,1,0:T(8,128)S(1)}, f32[16,64,128]{2,1,0:T(8,128)S(1)}, u32[]{:S(2)}, u32[]{:S(2)}) collective-permute-start(f32[16,64,128]{2,1,0:T(8,128)S(1)} %get-tuple-element.10), channel_id=1, source_target_pairs={{0,16},{8,24},{16,32},{24,40},{32,48},{40,56},{48,64},{56,72},{64,... | collective-permute-start | bytes 1572872 | tf_op jit(solution)/shard_map/ppermute | solution.py:168
  14.9 8.2 %collective-permute-start.2 = (f32[16,64,128]{2,1,0:T(8,128)S(1)}, f32[16,64,128]{2,1,0:T(8,128)S(1)}, u32[]{:S(2)}, u32[]{:S(2)}) collective-permute-start(f32[16,64,128]{2,1,0:T(8,128)S(1)} %get-tuple-element.11), channel_id=1, source_target_pairs={{0,176},{8,184},{16,0},{24,8},{32,16},{40,24},{48,32},{56,40},{64,... | collective-permute-start | bytes 1572872 | tf_op jit(solution)/shard_map/ppermute | solution.py:169
  23.1 10.3 %collective-permute-done.1 = f32[16,64,128]{2,1,0:T(8,128)S(1)} collective-permute-done((f32[16,64,128]{2,1,0:T(8,128)S(1)}, f32[16,64,128]{2,1,0:T(8,128)S(1)}, u32[]{:S(2)}, u32[]{:S(2)}) %collective-permute-start.1) | collective-permute-done | bytes 524320 | tf_op jit(solution)/shard_map/ppermute | solution.py:168
  33.4 1.2 %collective-permute-done.2 = f32[16,64,128]{2,1,0:T(8,128)S(1)} collective-permute-done((f32[16,64,128]{2,1,0:T(8,128)S(1)}, f32[16,64,128]{2,1,0:T(8,128)S(1)}, u32[]{:S(2)}, u32[]{:S(2)}) %collective-permute-start.2) | collective-permute-done | bytes 524320 | tf_op jit(solution)/shard_map/ppermute | solution.py:169
  34.6 0.1 fusion.1
  34.7 40.1 %all_to_all.10.parts = f32[16,64,128]{2,1,0:T(8,128)} all-to-all(f32[16,64,128]{2,1,0:T(8,128)S(1)} %fusion.1), channel_id=1, replica_groups={{0,192,384,576,48,240,432,624,96,288,480,672,144,336,528,720},{8,200,39..., dimensions={0} | all-to-all | bytes 1048576 | tf_op jit(solution)/shard_map/all_to_all | solution.py:171
  74.8 2.2 %shard_map.87 = (f32[64,128]{1,0:T(8,128)}, f32[8,8,128]{2,1,0:T(8,128)}) custom-call(f32[16,64,128]{2,1,0:T(8,128)} %all_to_all.10.parts, f32[1,2,4096]{2,1,0:T(2,128)} %momentum.1, s32[2,2]{1,0:T(2,128)} %corner.1, f32[64,64]{1,0:T(8,128)} %constant.8.clone.left, f32[128,128]{1,0:T(8,128)} %constant.10.clone.right), custom_call_target="tpu_custom_call" | custom-call | tf_op jit(solution)/shard_map/pallas_call | solution.py:173
  77.0 4.8 %all-to-all-start.1 = ((f32[8,8,128]{2,1,0:T(8,128)}), f32[8,8,128]{2,1,0:T(8,128)S(1)}, u32[]{:S(2)}, u32[]{:S(2)}) async-start(f32[8,8,128]{2,1,0:T(8,128)} %get-tuple-element.9.packed), calls=%async_computation.1 | async-start | bytes 65536 | tf_op jit(solution)/shard_map/all_to_all | solution.py:183
  81.8 2.0 %shard_map.88 = f32[1,2,4096]{2,1,0:T(2,128)} custom-call(f32[64,128]{1,0:T(8,128)} %get-tuple-element.8.moment, f32[8,8,128]{2,1,0:T(8,128)} %get-tuple-element.9.packed, f32[64,64]{1,0:T(8,128)} %constant.9.clone.left_t, f32[128,128]{1,0:T(8,128)} %constant.11.clone.right_t), custom_call_target="tpu_custom_call" | custom-call | tf_op jit(solution)/shard_map/pallas_call | solution.py:184
  83.7 4.3 %all-to-all-done.1.packed = f32[8,8,128]{2,1,0:T(8,128)S(1)} async-done(((f32[8,8,128]{2,1,0:T(8,128)}), f32[8,8,128]{2,1,0:T(8,128)S(1)}, u32[]{:S(2)}, u32[]{:S(2)}) %all-to-all-start.1) | async-done | bytes 32800 | tf_op jit(solution)/shard_map/all_to_all | solution.py:183
  88.0 0.0 copy-start.1
  88.0 0.6 copy-done.1
  88.6 2.0 %shard_map.89 = f32[2,4096]{1,0:T(2,128)} custom-call(f32[8,8,128]{2,1,0:T(8,128)} %copy-done.1, f32[64,64]{1,0:T(8,128)} %constant.9.clone.left_t, f32[128,128]{1,0:T(8,128)} %constant.11.clone.right_t), custom_call_target="tpu_custom_call" | custom-call | tf_op jit(solution)/shard_map/pallas_call | solution.py:191
Async XLA Ops:
  0.6 1.4 %copy-start = (bf16[1,1,192,4096]{3,2,1,0:T(8,128)(2,1)S(1)}, bf16[1,1,192,4096]{3,2,1,0:T(8,128)(2,1)}, u32[]{:S(2)}) copy-start(bf16[1,1,192,4096]{3,2,1,0:T(8,128)(2,1)} %grads.1) | copy-start | bytes 4718596
  4.9 5.3 %collective-permute-start = (f32[3,16,64,128]{3,2,1,0:T(8,128)S(1)}, f32[3,16,64,128]{3,2,1,0:T(8,128)S(1)}, u32[]{:S(2)}, u32[]{:S(2)}) collective-permute-start(f32[3,16,64,128]{3,2,1,0:T(8,128)S(1)} %get-tuple-element.7), channel_id=1, source_target_pairs={{0,8},{8,0},{16,24},{24,16},{32,40},{40,32},{48,56},{56,48},{64,72... | collective-permute-start | bytes 4718600 | tf_op jit(solution)/shard_map/ppermute | solution.py:167
  10.6 22.8 %collective-permute-start.1 = (f32[16,64,128]{2,1,0:T(8,128)S(1)}, f32[16,64,128]{2,1,0:T(8,128)S(1)}, u32[]{:S(2)}, u32[]{:S(2)}) collective-permute-start(f32[16,64,128]{2,1,0:T(8,128)S(1)} %get-tuple-element.10), channel_id=1, source_target_pairs={{0,16},{8,24},{16,32},{24,40},{32,48},{40,56},{48,64},{56,72},{64,... | collective-permute-start | bytes 1572872 | tf_op jit(solution)/shard_map/ppermute | solution.py:168
  14.9 19.7 %collective-permute-start.2 = (f32[16,64,128]{2,1,0:T(8,128)S(1)}, f32[16,64,128]{2,1,0:T(8,128)S(1)}, u32[]{:S(2)}, u32[]{:S(2)}) collective-permute-start(f32[16,64,128]{2,1,0:T(8,128)S(1)} %get-tuple-element.11), channel_id=1, source_target_pairs={{0,176},{8,184},{16,0},{24,8},{32,16},{40,24},{48,32},{56,40},{64,... | collective-permute-start | bytes 1572872 | tf_op jit(solution)/shard_map/ppermute | solution.py:169
  77.0 11.1 %all-to-all-start.1 = ((f32[8,8,128]{2,1,0:T(8,128)}), f32[8,8,128]{2,1,0:T(8,128)S(1)}, u32[]{:S(2)}, u32[]{:S(2)}) async-start(f32[8,8,128]{2,1,0:T(8,128)} %get-tuple-element.9.packed), calls=%async_computation.1 | async-start | bytes 65536 | tf_op jit(solution)/shard_map/all_to_all | solution.py:183
  88.0 0.6 copy-start.1

commit v2 on v0

v2 whole, which is shorter than its diff:
```python
import math

import jax
import jax.numpy as jnp
import ml_dtypes
import numpy as np
from jax import lax
from jax.experimental import pallas as pl
from jax.experimental.pallas import tpu as pltpu
from jax.sharding import PartitionSpec as P

SPAN = 64
CORNER = 8
LOW = 16
NY, NZ = 4, 12
N_DP = 96
N_OUTER = 8
VMEM = pl.BlockSpec(memory_space=pltpu.VMEM)
SMEM = pl.BlockSpec(memory_space=pltpu.SMEM)


def device_of(y, z, core):
    return ((y % NY) * NZ + z % NZ) * 2 + core


def shift(dz=0, dcore=0):
    return [
        (device_of(y, z, c), device_of(y, z + dz, c ^ dcore))
        for y in range(NY)
        for z in range(NZ)
        for c in range(2)
    ]


def y_groups():
    return [[device_of(y, z, c) for y in range(NY)] for z in range(NZ) for c in range(2)]


def z_groups():
    return [
        [device_of(y, 3 * q + s, c) for q in range(4)]
        for s in range(3)
        for y in range(NY)
        for c in range(2)
    ]


def halves(table):
    high = table.astype(ml_dtypes.bfloat16)
    low = (table - high.astype(np.float64)).astype(ml_dtypes.bfloat16)
    return high, low


def left_three(table):
    high, low = halves(table)
    return np.concatenate([high, low, high], axis=1)


def right_three(table):
    high, low = halves(table)
    return np.concatenate([high, low, high], axis=0)


def tables():
    k = np.arange(SPAN)[:, None]
    n = np.arange(SPAN)[None, :]
    scale = np.where(k == 0, math.sqrt(1.0 / SPAN), math.sqrt(2.0 / SPAN))
    low = (scale * np.cos(np.pi * (2 * n + 1) * k / (2.0 * SPAN)))[:LOW]
    left = np.zeros((2, 2, LOW, 2, 32))
    for h in range(2):
        for b in range(2):
            left[h, b, :, b, :] = low[:, h::2]
    left = left.reshape(64, 64)
    right = np.zeros((4, 128, 128))
    for g in range(4):
        right[g, :, 16 * g : 16 * g + 16] = np.concatenate([low.T, low.T], axis=0)
    right = right.reshape(512, 128)
    return left_three(left), right_three(right), left_three(left.T), right_three(right.T)


def chunk(y, q, kind, core):
    return pl.multiple_of(((y * NZ + 3 * q + kind) * 2 + core) * 64, 64)


def place():
    me = lax.axis_index("dp")
    core = lax.rem(me, 2)
    z = lax.rem(me // 2, NZ)
    return core, [lax.rem(z + d, 3) for d in (1, 2, 0)]


def arrange_kernel(grads, send, square):
    core, kinds = place()

    def spread(i, carry):
        rows = pl.multiple_of(i * 16, 16)
        for t in range(32):
            tile = grads[0, 0, pl.ds(rows, 16), t * 128 : (t + 1) * 128].astype(jnp.float32)
            square[pl.ds(rows * 32 + t, 16, stride=32), :] = tile
        return carry

    lax.fori_loop(0, 12, spread, 0)

    def deal(i, carry):
        y, q = i // 4, lax.rem(i, 4)
        for slot, kind in enumerate(kinds):
            send[slot, i] = square[pl.ds(chunk(y, q, kind, 1 - core), 64), :]
        return carry

    lax.fori_loop(0, 16, deal, 0)


def arrange(grads):
    shapes = [(3, 16, 64, 128), (6144, 128)]
    return pl.pallas_call(
        arrange_kernel,
        out_shape=tuple(jax.ShapeDtypeStruct(s, jnp.float32) for s in shapes),
        in_specs=[VMEM],
        out_specs=(VMEM, VMEM),
        compiler_params=pltpu.CompilerParams(vmem_limit_bytes=24 << 20),
    )(grads)


def chip_kernel(square, other, up, down, here):
    core, kinds = place()

    def add(i, carry):
        y, q = i // 4, lax.rem(i, 4)
        for slot, ref in enumerate((up, down, here)):
            mine = square[pl.ds(chunk(y, q, kinds[slot], core), 64), :]
            ref[i] = mine + other[slot, i]
        return carry

    lax.fori_loop(0, 16, add, 0)


def dot(a, b):
    return jnp.dot(a, b, preferred_element_type=jnp.float32)


def split(value):
    high = value.astype(jnp.bfloat16)
    low = (value - high.astype(jnp.float32)).astype(jnp.bfloat16)
    return high, low


def dot_left(table, value):
    high, low = split(value)
    return dot(table, jnp.concatenate([high, high, low], axis=0))


def dot_right(value, table):
    high, low = split(value)
    return dot(jnp.concatenate([high, high, low], axis=1), table)


def kept_kernel(parts, momentum, corner, left, right, moment, kept, copies, square):
    for t in range(32):
        square[pl.ds(t, 2, stride=32), :] = momentum[0, :, t * 128 : (t + 1) * 128]
    total = (parts[0] + parts[1]) + (parts[2] + parts[3])
    value = 0.9 * square[...] + total / N_DP
    moment[...] = value
    mixed = dot_left(left[...], value)
    lane = lax.broadcasted_iota(jnp.int32, (32, 128), 1)
    half = jnp.where(lane < SPAN, mixed[:32], mixed[32:])
    wide = jnp.concatenate([half[8 * g : 8 * g + 8] for g in range(4)], axis=1)
    low = dot_right(wide, right[...])
    row = lax.broadcasted_iota(jnp.int32, (8, 128), 0)
    lane = lax.broadcasted_iota(jnp.int32, (8, 128), 1)
    first = lane < 2 * LOW
    above = row + 8 * ((lane // LOW) % 2) - jnp.where(first, corner[0, 0], corner[1, 0])
    beside = lane % LOW - jnp.where(first, corner[0, 1], corner[1, 1])
    inside = (above >= 0) & (above < CORNER) & (beside >= 0) & (beside < CORNER)
    pack = jnp.where(inside & (lane < 4 * LOW), low, 0.0)
    kept[...] = pack
    for p in range(N_OUTER):
        copies[p] = pack


def last_kernel(moment, kept, packed, left_t, right_t, out, update, square, other):
    shared = packed[0]
    for p in range(1, N_OUTER):
        shared = shared + packed[p]
    both = jnp.concatenate([kept[...], shared / N_OUTER], axis=0)
    wide = dot_right(both, right_t[...])
    row = lax.broadcasted_iota(jnp.int32, (64, 128), 0)
    lane = lax.broadcasted_iota(jnp.int32, (64, 128), 1)
    same = (row < 32) == (lane < SPAN)
    sides = []
    for first in (0, 8):
        tall = [wide[first : first + 8, 128 * g : 128 * g + 128] for g in range(4)]
        sides.append(jnp.where(same, jnp.concatenate(tall + tall, axis=0), 0.0))
    back = dot_left(left_t[...], jnp.concatenate(sides, axis=1))
    square[...] = moment[...] - back[:, :128]
    other[...] = back[:, 128:]
    for t in range(32):
        out[0, :, t * 128 : (t + 1) * 128] = square[pl.ds(t, 2, stride=32), :]
        update[:, t * 128 : (t + 1) * 128] = other[pl.ds(t, 2, stride=32), :]


def call(kernel, out_shapes, args, scratch=(), smem=()):
    return pl.pallas_call(
        kernel,
        out_shape=tuple(jax.ShapeDtypeStruct(s, jnp.float32) for s in out_shapes),
        in_specs=[SMEM if i in smem else VMEM for i in range(len(args))],
        out_specs=tuple(VMEM for _ in out_shapes),
        scratch_shapes=[pltpu.VMEM(s, jnp.float32) for s in scratch],
        compiler_params=pltpu.CompilerParams(vmem_limit_bytes=24 << 20),
    )(*args)


def exchange(value, axis, groups=None):
    return lax.all_to_all(value, axis, 0, 0, axis_index_groups=groups, tiled=True)


def on_device(grads, momentum, corner):
    left, right, left_t, right_t = (jnp.asarray(v) for v in tables())
    tile = (64, 128)
    send, square = arrange(grads)
    other = lax.ppermute(send, "dp", shift(dcore=1))
    up, down, here = call(chip_kernel, [(16, 64, 128)] * 3, (square, other))
    from_below = lax.ppermute(up, "dp", shift(dz=1))
    from_above = lax.ppermute(down, "dp", shift(dz=-1))
    near = exchange(here + from_below + from_above, "dp", y_groups())
    line = near.reshape(NY, 4, 64, 128).sum(axis=0)
    parts = exchange(line, "dp", z_groups())
    moment, kept, copies = call(
        kept_kernel,
        [tile, (8, 128), (N_OUTER, 8, 128)],
        (parts, momentum, corner, left, right),
        [tile],
        smem=(2,),
    )
    packed = exchange(copies, "outer")
    return call(
        last_kernel,
        [(1, 2, 4096), (2, 4096)],
        (moment, kept, packed, left_t, right_t),
        [tile, tile],
    )


def solution(mesh):
    in_specs = (P("outer", "dp", None, None), P("outer", "dp", None), P("dp", None))
    out_specs = (P("outer", "dp", None), P("dp", None))
    return jax.shard_map(
        on_device, mesh=mesh, in_specs=in_specs, out_specs=out_specs, check_vma=False
    )
```

time: 889 us -> 90.9 us (0.10)
  the two profiles are of different devices: /device:TPU:8 before, /device:TPU:16 now
where the time goes in v2:
time: 90.9 us; the launch traced here: 90.6 us
  blocking collectives  50.1 us (55%)
  starting transfers between devices  18.4 us (20%)
  waiting for transfers between devices  14.8 us (16%)
  Pallas kernels  4.96 us (5%)
  local copies, waits for them, and re-layouts  1.43 us (2%)
    all_to_all x3, blocking collectives, exchange(): lax.all_to_all(value, axis, 0, 0, axis_index_groups=groups, tiled=True)  50.1 us
    ppermute x1, starting transfers between devices, on_device(): from_above = lax.ppermute(down, 'dp', shift(dz=-1))  12.2 us
    ppermute x1, waiting for transfers between devices, on_device(): from_below = lax.ppermute(up, 'dp', shift(dz=1))  10.3 us
    ppermute x1, starting transfers between devices, on_device(): from_below = lax.ppermute(up, 'dp', shift(dz=1))  4.28 us
    ppermute x1, waiting for transfers between devices, on_device(): other = lax.ppermute(send, 'dp', shift(dcore=1))  3.38 us
    pallas_call x1, Pallas kernels, arrange(): pl.pallas_call(arrange_kernel, out_shape=tuple((jax.ShapeDtypeStruct(s, j...  2.77 us
    pallas_call x3, Pallas kernels, call(): pl.pallas_call(kernel, out_shape=tuple((jax.ShapeDtypeStruct(s, jnp.float...  2.19 us
    ppermute x1, starting transfers between devices, on_device(): other = lax.ppermute(send, 'dp', shift(dcore=1))  1.92 us
  transfers between devices with their start and end apart: 3, of which 3 were waited for; matrix products, arithmetic and copies ran while one was open for 0% of the time, Pallas kernels for 0%

profile of v2, /device:TPU:16, one launch (start us, length us, event | category | flops | bytes accessed | tf_op | source)
XLA Modules:
  0.0 90.6 jit_solution(2681789504720327795)
XLA Ops:
  0.6 0.0 copy-start
  0.6 1.4 %copy-done = bf16[1,1,192,4096]{3,2,1,0:T(8,128)(2,1)S(1)} copy-done((bf16[1,1,192,4096]{3,2,1,0:T(8,128)(2,1)S(1)}, bf16[1,1,192,4096]{3,2,1,0:T(8,128)(2,1)}, u32[]{:S(2)}) %copy-start) | copy-done | bytes 1572888
  2.0 2.8 %shard_map.86 = (f32[3,16,64,128]{3,2,1,0:T(8,128)S(1)}, f32[6144,128]{1,0:T(8,128)S(1)}) custom-call(bf16[1,1,192,4096]{3,2,1,0:T(8,128)(2,1)S(1)} %copy-done), custom_call_target="tpu_custom_call" | custom-call | tf_op jit(solution)/shard_map/pallas_call | solution.py:115
  4.8 1.9 %collective-permute-start = (f32[3,16,64,128]{3,2,1,0:T(8,128)S(1)}, f32[3,16,64,128]{3,2,1,0:T(8,128)S(1)}, u32[]{:S(2)}, u32[]{:S(2)}) collective-permute-start(f32[3,16,64,128]{3,2,1,0:T(8,128)S(1)} %get-tuple-element.11), channel_id=1, source_target_pairs={{0,8},{8,0},{16,24},{24,16},{32,40},{40,32},{48,56},{56,48},{64,72... | collective-permute-start | bytes 4718600 | tf_op jit(solution)/shard_map/ppermute | solution.py:220
  6.7 3.4 %collective-permute-done.other = f32[3,16,64,128]{3,2,1,0:T(8,128)S(1)} collective-permute-done((f32[3,16,64,128]{3,2,1,0:T(8,128)S(1)}, f32[3,16,64,128]{3,2,1,0:T(8,128)S(1)}, u32[]{:S(2)}, u32[]{:S(2)}) %collective-permute-start) | collective-permute-done | bytes 1572896 | tf_op jit(solution)/shard_map/ppermute | solution.py:220
  10.1 0.3 shard_map.87
  10.4 4.3 %collective-permute-start.1 = (f32[16,64,128]{2,1,0:T(8,128)S(1)}, f32[16,64,128]{2,1,0:T(8,128)S(1)}, u32[]{:S(2)}, u32[]{:S(2)}) collective-permute-start(f32[16,64,128]{2,1,0:T(8,128)S(1)} %get-tuple-element.13), channel_id=1, source_target_pairs={{0,16},{8,24},{16,32},{24,40},{32,48},{40,56},{48,64},{56,72},{64,... | collective-permute-start | bytes 1572872 | tf_op jit(solution)/shard_map/ppermute | solution.py:222
  14.7 12.2 %collective-permute-start.2 = (f32[16,64,128]{2,1,0:T(8,128)S(1)}, f32[16,64,128]{2,1,0:T(8,128)S(1)}, u32[]{:S(2)}, u32[]{:S(2)}) collective-permute-start(f32[16,64,128]{2,1,0:T(8,128)S(1)} %get-tuple-element.14), channel_id=1, source_target_pairs={{0,176},{8,184},{16,0},{24,8},{32,16},{40,24},{48,32},{56,40},{64,... | collective-permute-start | bytes 1572872 | tf_op jit(solution)/shard_map/ppermute | solution.py:223
  26.9 10.3 %collective-permute-done.1 = f32[16,64,128]{2,1,0:T(8,128)S(1)} collective-permute-done((f32[16,64,128]{2,1,0:T(8,128)S(1)}, f32[16,64,128]{2,1,0:T(8,128)S(1)}, u32[]{:S(2)}, u32[]{:S(2)}) %collective-permute-start.1) | collective-permute-done | bytes 524320 | tf_op jit(solution)/shard_map/ppermute | solution.py:222
  37.2 1.2 %collective-permute-done.2 = f32[16,64,128]{2,1,0:T(8,128)S(1)} collective-permute-done((f32[16,64,128]{2,1,0:T(8,128)S(1)}, f32[16,64,128]{2,1,0:T(8,128)S(1)}, u32[]{:S(2)}, u32[]{:S(2)}) %collective-permute-start.2) | collective-permute-done | bytes 524320 | tf_op jit(solution)/shard_map/ppermute | solution.py:223
  38.4 0.0 copy-start.1
  38.4 0.0 copy-start.3
  38.4 0.0 copy-start.4
  38.4 0.0 copy-start.6
  38.4 0.1 add_add_fusion
  38.5 0.0 copy-start.2
  38.5 0.0 copy-start.5
  38.5 21.8 %all_to_all.15 = f32[16,64,128]{2,1,0:T(8,128)S(1)} all-to-all(f32[16,64,128]{2,1,0:T(8,128)S(1)} %add_add_fusion), channel_id=1, replica_groups={{0,192,384,576},{8,200,392,584},{16,208,400,592},{24,216,408,600},{32,2..., dimensions={0} | all-to-all | bytes 1048576 | tf_op jit(solution)/shard_map/all_to_all | solution.py:213
  60.3 18.0 %all_to_all.16.parts = f32[4,64,128]{2,1,0:T(8,128)S(1)} all-to-all(f32[4,64,128]{2,1,0:T(8,128)S(1)} %reduce_sum.9), channel_id=1, replica_groups={{0,48,96,144},{8,56,104,152},{192,240,288,336},{200,248,296,344},{384,4..., dimensions={0} | all-to-all | bytes 262144 | tf_op jit(solution)/shard_map/all_to_all | solution.py:213
  78.3 0.0 copy-done.1
  78.3 0.0 copy-done.3
  78.3 0.0 copy-done.4
  78.3 0.0 copy-done.6
  78.3 0.9 shard_map.88
  79.2 10.4 %all_to_all.17.packed = f32[8,8,128]{2,1,0:T(8,128)S(1)} all-to-all(f32[8,8,128]{2,1,0:T(8,128)S(1)} %get-tuple-element.17), channel_id=1, replica_groups=mesh['dp'=96,'outer'=8] {'outer'}, dimensions={0} | all-to-all | bytes 65536 | tf_op jit(solution)/shard_map/all_to_all | solution.py:213
  89.6 0.0 copy-done.2
  89.6 0.0 copy-done.5
  89.6 1.0 %shard_map.89 = (f32[1,2,4096]{2,1,0:T(2,128)}, f32[2,4096]{1,0:T(2,128)}) custom-call(f32[64,128]{1,0:T(8,128)S(1)} %get-tuple-element.15.moment, f32[8,128]{1,0:T(8,128)S(1)} %get-tuple-element.16.kept, f32[8,8,128]{2,1,0:T(8,128)S(1)} %all_to_all.17.packed, bf16[64,192]{1,0:T(8,128)(2,1)S(1)} %copy-done.5, bf16[384,512]{1,0:T(8,128)(2,1)S(1)} %copy-done.2), custom_call_target="tpu_custom_call" | custom-call | tf_op jit(solution)/shard_map/pallas_call | solution.py:202
  (1 shorter events, 0.0 us)
Async XLA Ops:
  0.6 1.4 %copy-start = (bf16[1,1,192,4096]{3,2,1,0:T(8,128)(2,1)S(1)}, bf16[1,1,192,4096]{3,2,1,0:T(8,128)(2,1)}, u32[]{:S(2)}) copy-start(bf16[1,1,192,4096]{3,2,1,0:T(8,128)(2,1)} %grads.1) | copy-start | bytes 4718596
  4.8 5.3 %collective-permute-start = (f32[3,16,64,128]{3,2,1,0:T(8,128)S(1)}, f32[3,16,64,128]{3,2,1,0:T(8,128)S(1)}, u32[]{:S(2)}, u32[]{:S(2)}) collective-permute-start(f32[3,16,64,128]{3,2,1,0:T(8,128)S(1)} %get-tuple-element.11), channel_id=1, source_target_pairs={{0,8},{8,0},{16,24},{24,16},{32,40},{40,32},{48,56},{56,48},{64,72... | collective-permute-start | bytes 4718600 | tf_op jit(solution)/shard_map/ppermute | solution.py:220
  10.4 26.8 %collective-permute-start.1 = (f32[16,64,128]{2,1,0:T(8,128)S(1)}, f32[16,64,128]{2,1,0:T(8,128)S(1)}, u32[]{:S(2)}, u32[]{:S(2)}) collective-permute-start(f32[16,64,128]{2,1,0:T(8,128)S(1)} %get-tuple-element.13), channel_id=1, source_target_pairs={{0,16},{8,24},{16,32},{24,40},{32,48},{40,56},{48,64},{56,72},{64,... | collective-permute-start | bytes 1572872 | tf_op jit(solution)/shard_map/ppermute | solution.py:222
  14.7 23.7 %collective-permute-start.2 = (f32[16,64,128]{2,1,0:T(8,128)S(1)}, f32[16,64,128]{2,1,0:T(8,128)S(1)}, u32[]{:S(2)}, u32[]{:S(2)}) collective-permute-start(f32[16,64,128]{2,1,0:T(8,128)S(1)} %get-tuple-element.14), channel_id=1, source_target_pairs={{0,176},{8,184},{16,0},{24,8},{32,16},{40,24},{48,32},{56,40},{64,... | collective-permute-start | bytes 1572872 | tf_op jit(solution)/shard_map/ppermute | solution.py:223
  38.4 39.9 %copy-start.1 = (bf16[1536,128]{1,0:T(8,128)(2,1)S(1)}, bf16[1536,128]{1,0:T(8,128)(2,1)}, u32[]{:S(2)}) copy-start(bf16[1536,128]{1,0:T(8,128)(2,1)} %constant.11.clone.right) | copy-start | bytes 1179652
  38.4 39.9 %copy-start.3 = (f32[1,2,4096]{2,1,0:T(2,128)S(1)}, f32[1,2,4096]{2,1,0:T(2,128)}, u32[]{:S(2)}) copy-start(f32[1,2,4096]{2,1,0:T(2,128)} %momentum.1) | copy-start | bytes 98308
  38.4 39.9 %copy-start.4 = (bf16[64,192]{1,0:T(8,128)(2,1)S(1)}, bf16[64,192]{1,0:T(8,128)(2,1)}, u32[]{:S(2)}) copy-start(bf16[64,192]{1,0:T(8,128)(2,1)} %constant.10.clone.left) | copy-start | bytes 73732
  38.4 39.9 %copy-start.6 = (s32[2,2]{1,0:T(2,128)S(1)}, s32[2,2]{1,0:T(2,128)}, u32[]{:S(2)}) copy-start(s32[2,2]{1,0:T(2,128)} %corner.1) | copy-start | bytes 52
  38.5 51.1 %copy-start.2 = (bf16[384,512]{1,0:T(8,128)(2,1)S(1)}, bf16[384,512]{1,0:T(8,128)(2,1)}, u32[]{:S(2)}) copy-start(bf16[384,512]{1,0:T(8,128)(2,1)} %constant.13.clone.right_t) | copy-start | bytes 1179652
  38.5 51.1 %copy-start.5 = (bf16[64,192]{1,0:T(8,128)(2,1)S(1)}, bf16[64,192]{1,0:T(8,128)(2,1)}, u32[]{:S(2)}) copy-start(bf16[64,192]{1,0:T(8,128)(2,1)} %constant.12.clone.left_t) | copy-start | bytes 73732

commit v3 on v2

--- a/solution.py
+++ b/solution.py
@@ -25,7 +25,7 @@
 
 def shift(dz=0, dcore=0):
     return [
-        (device_of(y, z, c), device_of(y, z + dz, c ^ dcore))
+        (device_of(y, z, c), device_of(y, z + dz * (1 - 2 * c), c ^ dcore))
         for y in range(NY)
         for z in range(NZ)
         for c in range(2)
@@ -86,7 +86,7 @@
     me = lax.axis_index("dp")
     core = lax.rem(me, 2)
     z = lax.rem(me // 2, NZ)
-    return core, [lax.rem(z + d, 3) for d in (1, 2, 0)]
+    return core, [lax.rem(z + d, 3) for d in (1 + core, 2 - core, 0)]
 
 
 def arrange_kernel(grads, send, square):
@@ -103,7 +103,7 @@
 
     def deal(i, carry):
         y, q = i // 4, lax.rem(i, 4)
-        for slot, kind in enumerate(kinds):
+        for slot, kind in enumerate((kinds[1], kinds[0], kinds[2])):
             send[slot, i] = square[pl.ds(chunk(y, q, kind, 1 - core), 64), :]
         return carry
 
@@ -121,12 +121,12 @@
     )(grads)
 
 
-def chip_kernel(square, other, up, down, here):
+def chip_kernel(square, other, first, second, here):
     core, kinds = place()
 
     def add(i, carry):
         y, q = i // 4, lax.rem(i, 4)
-        for slot, ref in enumerate((up, down, here)):
+        for slot, ref in enumerate((first, second, here)):
             mine = square[pl.ds(chunk(y, q, kinds[slot], core), 64), :]
             ref[i] = mine + other[slot, i]
         return carry
@@ -218,10 +218,10 @@
     tile = (64, 128)
     send, square = arrange(grads)
     other = lax.ppermute(send, "dp", shift(dcore=1))
-    up, down, here = call(chip_kernel, [(16, 64, 128)] * 3, (square, other))
-    from_below = lax.ppermute(up, "dp", shift(dz=1))
-    from_above = lax.ppermute(down, "dp", shift(dz=-1))
-    near = exchange(here + from_below + from_above, "dp", y_groups())
+    first, second, here = call(chip_kernel, [(16, 64, 128)] * 3, (square, other))
+    one = lax.ppermute(first, "dp", shift(dz=1))
+    two = lax.ppermute(second, "dp", shift(dz=-1))
+    near = exchange(here + one + two, "dp", y_groups())
     line = near.reshape(NY, 4, 64, 128).sum(axis=0)
     parts = exchange(line, "dp", z_groups())
     moment, kept, copies = call(

time: 90.9 us -> 89.5 us (0.985)
  waiting for transfers between devices: 14.8 us -> 12.9 us
    ppermute x2, waiting for transfers between devices: 11.5 us -> 9.53 us  [the longest x1 6.74 us: on_device(): one = lax.ppermute(first, 'dp', shift(dz=1))]
where the time goes in v3:
time: 89.5 us; the launch traced here: 89.2 us
  blocking collectives  50.6 us (57%)
  starting transfers between devices  18.4 us (21%)
  waiting for transfers between devices  12.9 us (14%)
  Pallas kernels  4.96 us (6%)
  local copies, waits for them, and re-layouts  1.43 us (2%)
    all_to_all x3, blocking collectives, exchange(): lax.all_to_all(value, axis, 0, 0, axis_index_groups=groups, tiled=True)  50.6 us
    ppermute x1, starting transfers between devices, on_device(): two = lax.ppermute(second, 'dp', shift(dz=-1))  12.2 us
    ppermute x1, waiting for transfers between devices, on_device(): one = lax.ppermute(first, 'dp', shift(dz=1))  6.74 us
    ppermute x1, starting transfers between devices, on_device(): one = lax.ppermute(first, 'dp', shift(dz=1))  4.28 us
    ppermute x1, waiting for transfers between devices, on_device(): other = lax.ppermute(send, 'dp', shift(dcore=1))  3.38 us
    ppermute x1, waiting for transfers between devices, on_device(): two = lax.ppermute(second, 'dp', shift(dz=-1))  2.8 us
    pallas_call x1, Pallas kernels, arrange(): pl.pallas_call(arrange_kernel, out_shape=tuple((jax.ShapeDtypeStruct(s, j...  2.77 us
    pallas_call x3, Pallas kernels, call(): pl.pallas_call(kernel, out_shape=tuple((jax.ShapeDtypeStruct(s, jnp.float...  2.19 us
  transfers between devices with their start and end apart: 3, of which 3 were waited for; matrix products, arithmetic and copies ran while one was open for 0% of the time, Pallas kernels for 0%

profile of v3, /device:TPU:16, one launch (start us, length us, event | category | flops | bytes accessed | tf_op | source)
XLA Modules:
  0.0 89.2 jit_solution(16764879543369915406)
XLA Ops:
  0.6 0.0 copy-start
  0.6 1.4 %copy-done = bf16[1,1,192,4096]{3,2,1,0:T(8,128)(2,1)S(1)} copy-done((bf16[1,1,192,4096]{3,2,1,0:T(8,128)(2,1)S(1)}, bf16[1,1,192,4096]{3,2,1,0:T(8,128)(2,1)}, u32[]{:S(2)}) %copy-start) | copy-done | bytes 1572888
  2.0 2.8 %shard_map.86 = (f32[3,16,64,128]{3,2,1,0:T(8,128)S(1)}, f32[6144,128]{1,0:T(8,128)S(1)}) custom-call(bf16[1,1,192,4096]{3,2,1,0:T(8,128)(2,1)S(1)} %copy-done), custom_call_target="tpu_custom_call" | custom-call | tf_op jit(solution)/shard_map/pallas_call | solution.py:115
  4.8 1.9 %collective-permute-start = (f32[3,16,64,128]{3,2,1,0:T(8,128)S(1)}, f32[3,16,64,128]{3,2,1,0:T(8,128)S(1)}, u32[]{:S(2)}, u32[]{:S(2)}) collective-permute-start(f32[3,16,64,128]{3,2,1,0:T(8,128)S(1)} %get-tuple-element.11), channel_id=1, source_target_pairs={{0,8},{8,0},{16,24},{24,16},{32,40},{40,32},{48,56},{56,48},{64,72... | collective-permute-start | bytes 4718600 | tf_op jit(solution)/shard_map/ppermute | solution.py:220
  6.7 3.4 %collective-permute-done.other = f32[3,16,64,128]{3,2,1,0:T(8,128)S(1)} collective-permute-done((f32[3,16,64,128]{3,2,1,0:T(8,128)S(1)}, f32[3,16,64,128]{3,2,1,0:T(8,128)S(1)}, u32[]{:S(2)}, u32[]{:S(2)}) %collective-permute-start) | collective-permute-done | bytes 1572896 | tf_op jit(solution)/shard_map/ppermute | solution.py:220
  10.1 0.3 shard_map.87
  10.4 4.3 %collective-permute-start.1 = (f32[16,64,128]{2,1,0:T(8,128)S(1)}, f32[16,64,128]{2,1,0:T(8,128)S(1)}, u32[]{:S(2)}, u32[]{:S(2)}) collective-permute-start(f32[16,64,128]{2,1,0:T(8,128)S(1)} %get-tuple-element.13), channel_id=1, source_target_pairs={{0,16},{8,184},{16,32},{24,8},{32,48},{40,24},{48,64},{56,40},{64,... | collective-permute-start | bytes 1572872 | tf_op jit(solution)/shard_map/ppermute | solution.py:222
  14.7 12.2 %collective-permute-start.2 = (f32[16,64,128]{2,1,0:T(8,128)S(1)}, f32[16,64,128]{2,1,0:T(8,128)S(1)}, u32[]{:S(2)}, u32[]{:S(2)}) collective-permute-start(f32[16,64,128]{2,1,0:T(8,128)S(1)} %get-tuple-element.14), channel_id=1, source_target_pairs={{0,176},{8,24},{16,0},{24,40},{32,16},{40,56},{48,32},{56,72},{64,... | collective-permute-start | bytes 1572872 | tf_op jit(solution)/shard_map/ppermute | solution.py:223
  26.9 6.7 %collective-permute-done.1 = f32[16,64,128]{2,1,0:T(8,128)S(1)} collective-permute-done((f32[16,64,128]{2,1,0:T(8,128)S(1)}, f32[16,64,128]{2,1,0:T(8,128)S(1)}, u32[]{:S(2)}, u32[]{:S(2)}) %collective-permute-start.1) | collective-permute-done | bytes 524320 | tf_op jit(solution)/shard_map/ppermute | solution.py:222
  33.7 2.8 %collective-permute-done.2 = f32[16,64,128]{2,1,0:T(8,128)S(1)} collective-permute-done((f32[16,64,128]{2,1,0:T(8,128)S(1)}, f32[16,64,128]{2,1,0:T(8,128)S(1)}, u32[]{:S(2)}, u32[]{:S(2)}) %collective-permute-start.2) | collective-permute-done | bytes 524320 | tf_op jit(solution)/shard_map/ppermute | solution.py:223
  36.5 0.0 copy-start.1
  36.5 0.0 copy-start.3
  36.5 0.0 copy-start.4
  36.5 0.0 copy-start.6
  36.5 0.1 add_add_fusion
  36.6 0.0 copy-start.2
  36.6 0.0 copy-start.5
  36.6 23.4 %all_to_all.15 = f32[16,64,128]{2,1,0:T(8,128)S(1)} all-to-all(f32[16,64,128]{2,1,0:T(8,128)S(1)} %add_add_fusion), channel_id=1, replica_groups={{0,192,384,576},{8,200,392,584},{16,208,400,592},{24,216,408,600},{32,2..., dimensions={0} | all-to-all | bytes 1048576 | tf_op jit(solution)/shard_map/all_to_all | solution.py:213
  60.1 16.9 %all_to_all.16.parts = f32[4,64,128]{2,1,0:T(8,128)S(1)} all-to-all(f32[4,64,128]{2,1,0:T(8,128)S(1)} %reduce_sum.9), channel_id=1, replica_groups={{0,48,96,144},{8,56,104,152},{192,240,288,336},{200,248,296,344},{384,4..., dimensions={0} | all-to-all | bytes 262144 | tf_op jit(solution)/shard_map/all_to_all | solution.py:213
  76.9 0.0 copy-done.1
  76.9 0.0 copy-done.3
  76.9 0.0 copy-done.4
  76.9 0.0 copy-done.6
  76.9 0.9 shard_map.88
  77.8 10.4 %all_to_all.17.packed = f32[8,8,128]{2,1,0:T(8,128)S(1)} all-to-all(f32[8,8,128]{2,1,0:T(8,128)S(1)} %get-tuple-element.17), channel_id=1, replica_groups=mesh['dp'=96,'outer'=8] {'outer'}, dimensions={0} | all-to-all | bytes 65536 | tf_op jit(solution)/shard_map/all_to_all | solution.py:213
  88.2 0.0 copy-done.2
  88.2 0.0 copy-done.5
  88.2 1.0 %shard_map.89 = (f32[1,2,4096]{2,1,0:T(2,128)}, f32[2,4096]{1,0:T(2,128)}) custom-call(f32[64,128]{1,0:T(8,128)S(1)} %get-tuple-element.15.moment, f32[8,128]{1,0:T(8,128)S(1)} %get-tuple-element.16.kept, f32[8,8,128]{2,1,0:T(8,128)S(1)} %all_to_all.17.packed, bf16[64,192]{1,0:T(8,128)(2,1)S(1)} %copy-done.5, bf16[384,512]{1,0:T(8,128)(2,1)S(1)} %copy-done.2), custom_call_target="tpu_custom_call" | custom-call | tf_op jit(solution)/shard_map/pallas_call | solution.py:202
  (1 shorter events, 0.0 us)
Async XLA Ops:
  0.6 1.4 %copy-start = (bf16[1,1,192,4096]{3,2,1,0:T(8,128)(2,1)S(1)}, bf16[1,1,192,4096]{3,2,1,0:T(8,128)(2,1)}, u32[]{:S(2)}) copy-start(bf16[1,1,192,4096]{3,2,1,0:T(8,128)(2,1)} %grads.1) | copy-start | bytes 4718596
  4.8 5.3 %collective-permute-start = (f32[3,16,64,128]{3,2,1,0:T(8,128)S(1)}, f32[3,16,64,128]{3,2,1,0:T(8,128)S(1)}, u32[]{:S(2)}, u32[]{:S(2)}) collective-permute-start(f32[3,16,64,128]{3,2,1,0:T(8,128)S(1)} %get-tuple-element.11), channel_id=1, source_target_pairs={{0,8},{8,0},{16,24},{24,16},{32,40},{40,32},{48,56},{56,48},{64,72... | collective-permute-start | bytes 4718600 | tf_op jit(solution)/shard_map/ppermute | solution.py:220
  10.4 23.3 %collective-permute-start.1 = (f32[16,64,128]{2,1,0:T(8,128)S(1)}, f32[16,64,128]{2,1,0:T(8,128)S(1)}, u32[]{:S(2)}, u32[]{:S(2)}) collective-permute-start(f32[16,64,128]{2,1,0:T(8,128)S(1)} %get-tuple-element.13), channel_id=1, source_target_pairs={{0,16},{8,184},{16,32},{24,8},{32,48},{40,24},{48,64},{56,40},{64,... | collective-permute-start | bytes 1572872 | tf_op jit(solution)/shard_map/ppermute | solution.py:222
  14.7 21.8 %collective-permute-start.2 = (f32[16,64,128]{2,1,0:T(8,128)S(1)}, f32[16,64,128]{2,1,0:T(8,128)S(1)}, u32[]{:S(2)}, u32[]{:S(2)}) collective-permute-start(f32[16,64,128]{2,1,0:T(8,128)S(1)} %get-tuple-element.14), channel_id=1, source_target_pairs={{0,176},{8,24},{16,0},{24,40},{32,16},{40,56},{48,32},{56,72},{64,... | collective-permute-start | bytes 1572872 | tf_op jit(solution)/shard_map/ppermute | solution.py:223
  36.5 40.5 %copy-start.1 = (bf16[1536,128]{1,0:T(8,128)(2,1)S(1)}, bf16[1536,128]{1,0:T(8,128)(2,1)}, u32[]{:S(2)}) copy-start(bf16[1536,128]{1,0:T(8,128)(2,1)} %constant.11.clone.right) | copy-start | bytes 1179652
  36.5 40.5 %copy-start.3 = (f32[1,2,4096]{2,1,0:T(2,128)S(1)}, f32[1,2,4096]{2,1,0:T(2,128)}, u32[]{:S(2)}) copy-start(f32[1,2,4096]{2,1,0:T(2,128)} %momentum.1) | copy-start | bytes 98308
  36.5 40.5 %copy-start.4 = (bf16[64,192]{1,0:T(8,128)(2,1)S(1)}, bf16[64,192]{1,0:T(8,128)(2,1)}, u32[]{:S(2)}) copy-start(bf16[64,192]{1,0:T(8,128)(2,1)} %constant.10.clone.left) | copy-start | bytes 73732
  36.5 40.5 %copy-start.6 = (s32[2,2]{1,0:T(2,128)S(1)}, s32[2,2]{1,0:T(2,128)}, u32[]{:S(2)}) copy-start(s32[2,2]{1,0:T(2,128)} %corner.1) | copy-start | bytes 52
  36.6 51.6 %copy-start.2 = (bf16[384,512]{1,0:T(8,128)(2,1)S(1)}, bf16[384,512]{1,0:T(8,128)(2,1)}, u32[]{:S(2)}) copy-start(bf16[384,512]{1,0:T(8,128)(2,1)} %constant.13.clone.right_t) | copy-start | bytes 1179652
  36.6 51.6 %copy-start.5 = (bf16[64,192]{1,0:T(8,128)(2,1)S(1)}, bf16[64,192]{1,0:T(8,128)(2,1)}, u32[]{:S(2)}) copy-start(bf16[64,192]{1,0:T(8,128)(2,1)} %constant.12.clone.left_t) | copy-start | bytes 73732

commit v4 on v3

--- a/solution.py
+++ b/solution.py
@@ -94,9 +94,14 @@
 
     def spread(i, carry):
         rows = pl.multiple_of(i * 16, 16)
-        for t in range(32):
-            tile = grads[0, 0, pl.ds(rows, 16), t * 128 : (t + 1) * 128].astype(jnp.float32)
-            square[pl.ds(rows * 32 + t, 16, stride=32), :] = tile
+        for first in range(0, 32, 8):
+            wide = grads[0, 0, pl.ds(rows, 16), first * 128 : (first + 8) * 128]
+            wide = wide.astype(jnp.float32)
+            for side in (0, 8):
+                turned = wide[side : side + 8].reshape(8, 8, 128)
+                for r in range(8):
+                    start = pl.multiple_of((rows + side + r) * 32 + first, 8)
+                    square[pl.ds(start, 8), :] = turned[r]
         return carry
 
     lax.fori_loop(0, 12, spread, 0)

time: 89.5 us -> 87.7 us (0.980)
  Pallas kernels: 4.96 us -> 3.15 us
    pallas_call x1, Pallas kernels: 2.77 us -> 0.96 us  [arrange(): pl.pallas_call(arrange_kernel, out_shape=tuple((jax.ShapeDtypeStruct(s, j...]
where the time goes in v4:
time: 87.7 us; the launch traced here: 87.4 us
  blocking collectives  50.6 us (58%)
  starting transfers between devices  18.4 us (21%)
  waiting for transfers between devices  12.9 us (15%)
  Pallas kernels  3.15 us (4%)
  local copies, waits for them, and re-layouts  1.43 us (2%)
    all_to_all x3, blocking collectives, exchange(): lax.all_to_all(value, axis, 0, 0, axis_index_groups=groups, tiled=True)  50.6 us
    ppermute x1, starting transfers between devices, on_device(): two = lax.ppermute(second, 'dp', shift(dz=-1))  12.2 us
    ppermute x1, waiting for transfers between devices, on_device(): one = lax.ppermute(first, 'dp', shift(dz=1))  6.74 us
    ppermute x1, starting transfers between devices, on_device(): one = lax.ppermute(first, 'dp', shift(dz=1))  4.28 us
    ppermute x1, waiting for transfers between devices, on_device(): other = lax.ppermute(send, 'dp', shift(dcore=1))  3.38 us
    ppermute x1, waiting for transfers between devices, on_device(): two = lax.ppermute(second, 'dp', shift(dz=-1))  2.8 us
    pallas_call x3, Pallas kernels, call(): pl.pallas_call(kernel, out_shape=tuple((jax.ShapeDtypeStruct(s, jnp.float...  2.19 us
    ppermute x1, starting transfers between devices, on_device(): other = lax.ppermute(send, 'dp', shift(dcore=1))  1.92 us
  transfers between devices with their start and end apart: 3, of which 3 were waited for; matrix products, arithmetic and copies ran while one was open for 0% of the time, Pallas kernels for 0%

profile of v4, /device:TPU:16, one launch (start us, length us, event | category | flops | bytes accessed | tf_op | source)
XLA Modules:
  0.0 87.4 jit_solution(5542054475948706183)
XLA Ops:
  0.6 0.0 copy-start
  0.6 1.4 %copy-done = bf16[1,1,192,4096]{3,2,1,0:T(8,128)(2,1)S(1)} copy-done((bf16[1,1,192,4096]{3,2,1,0:T(8,128)(2,1)S(1)}, bf16[1,1,192,4096]{3,2,1,0:T(8,128)(2,1)}, u32[]{:S(2)}) %copy-start) | copy-done | bytes 1572888
  2.0 1.0 %shard_map.86 = (f32[3,16,64,128]{3,2,1,0:T(8,128)S(1)}, f32[6144,128]{1,0:T(8,128)S(1)}) custom-call(bf16[1,1,192,4096]{3,2,1,0:T(8,128)(2,1)S(1)} %copy-done), custom_call_target="tpu_custom_call" | custom-call | tf_op jit(solution)/shard_map/pallas_call | solution.py:120
  3.0 1.9 %collective-permute-start = (f32[3,16,64,128]{3,2,1,0:T(8,128)S(1)}, f32[3,16,64,128]{3,2,1,0:T(8,128)S(1)}, u32[]{:S(2)}, u32[]{:S(2)}) collective-permute-start(f32[3,16,64,128]{3,2,1,0:T(8,128)S(1)} %get-tuple-element.11), channel_id=1, source_target_pairs={{0,8},{8,0},{16,24},{24,16},{32,40},{40,32},{48,56},{56,48},{64,72... | collective-permute-start | bytes 4718600 | tf_op jit(solution)/shard_map/ppermute | solution.py:225
  4.9 3.4 %collective-permute-done.other = f32[3,16,64,128]{3,2,1,0:T(8,128)S(1)} collective-permute-done((f32[3,16,64,128]{3,2,1,0:T(8,128)S(1)}, f32[3,16,64,128]{3,2,1,0:T(8,128)S(1)}, u32[]{:S(2)}, u32[]{:S(2)}) %collective-permute-start) | collective-permute-done | bytes 1572896 | tf_op jit(solution)/shard_map/ppermute | solution.py:225
  8.3 0.3 shard_map.87
  8.6 4.3 %collective-permute-start.1 = (f32[16,64,128]{2,1,0:T(8,128)S(1)}, f32[16,64,128]{2,1,0:T(8,128)S(1)}, u32[]{:S(2)}, u32[]{:S(2)}) collective-permute-start(f32[16,64,128]{2,1,0:T(8,128)S(1)} %get-tuple-element.13), channel_id=1, source_target_pairs={{0,16},{8,184},{16,32},{24,8},{32,48},{40,24},{48,64},{56,40},{64,... | collective-permute-start | bytes 1572872 | tf_op jit(solution)/shard_map/ppermute | solution.py:227
  12.9 12.2 %collective-permute-start.2 = (f32[16,64,128]{2,1,0:T(8,128)S(1)}, f32[16,64,128]{2,1,0:T(8,128)S(1)}, u32[]{:S(2)}, u32[]{:S(2)}) collective-permute-start(f32[16,64,128]{2,1,0:T(8,128)S(1)} %get-tuple-element.14), channel_id=1, source_target_pairs={{0,176},{8,24},{16,0},{24,40},{32,16},{40,56},{48,32},{56,72},{64,... | collective-permute-start | bytes 1572872 | tf_op jit(solution)/shard_map/ppermute | solution.py:228
  25.1 6.7 %collective-permute-done.1 = f32[16,64,128]{2,1,0:T(8,128)S(1)} collective-permute-done((f32[16,64,128]{2,1,0:T(8,128)S(1)}, f32[16,64,128]{2,1,0:T(8,128)S(1)}, u32[]{:S(2)}, u32[]{:S(2)}) %collective-permute-start.1) | collective-permute-done | bytes 524320 | tf_op jit(solution)/shard_map/ppermute | solution.py:227
  31.9 2.8 %collective-permute-done.2 = f32[16,64,128]{2,1,0:T(8,128)S(1)} collective-permute-done((f32[16,64,128]{2,1,0:T(8,128)S(1)}, f32[16,64,128]{2,1,0:T(8,128)S(1)}, u32[]{:S(2)}, u32[]{:S(2)}) %collective-permute-start.2) | collective-permute-done | bytes 524320 | tf_op jit(solution)/shard_map/ppermute | solution.py:228
  34.7 0.0 copy-start.1
  34.7 0.0 copy-start.3
  34.7 0.0 copy-start.4
  34.7 0.0 copy-start.6
  34.7 0.1 add_add_fusion
  34.8 0.0 copy-start.2
  34.8 0.0 copy-start.5
  34.8 23.4 %all_to_all.15 = f32[16,64,128]{2,1,0:T(8,128)S(1)} all-to-all(f32[16,64,128]{2,1,0:T(8,128)S(1)} %add_add_fusion), channel_id=1, replica_groups={{0,192,384,576},{8,200,392,584},{16,208,400,592},{24,216,408,600},{32,2..., dimensions={0} | all-to-all | bytes 1048576 | tf_op jit(solution)/shard_map/all_to_all | solution.py:218
  58.2 16.9 %all_to_all.16.parts = f32[4,64,128]{2,1,0:T(8,128)S(1)} all-to-all(f32[4,64,128]{2,1,0:T(8,128)S(1)} %reduce_sum.9), channel_id=1, replica_groups={{0,48,96,144},{8,56,104,152},{192,240,288,336},{200,248,296,344},{384,4..., dimensions={0} | all-to-all | bytes 262144 | tf_op jit(solution)/shard_map/all_to_all | solution.py:218
  75.1 0.0 copy-done.1
  75.1 0.0 copy-done.3
  75.1 0.0 copy-done.4
  75.1 0.0 copy-done.6
  75.1 0.9 %shard_map.88 = (f32[64,128]{1,0:T(8,128)S(1)}, f32[8,128]{1,0:T(8,128)S(1)}, f32[8,8,128]{2,1,0:T(8,128)S(1)}) custom-call(f32[4,64,128]{2,1,0:T(8,128)S(1)} %all_to_all.16.parts, f32[1,2,4096]{2,1,0:T(2,128)S(1)} %copy-done.3, s32[2,2]{1,0:T(2,128)S(1)} %copy-done.6, bf16[64,192]{1,0:T(8,128)(2,1)S(1)} %copy-done.4, bf16[1536,128]{1,0:T(8,128)(2,1)S(1)} %copy-done.1), custom_call_target="tpu_custom_call" | custom-call | tf_op jit(solution)/shard_map/pallas_call | solution.py:207
  76.0 10.4 %all_to_all.17.packed = f32[8,8,128]{2,1,0:T(8,128)S(1)} all-to-all(f32[8,8,128]{2,1,0:T(8,128)S(1)} %get-tuple-element.17), channel_id=1, replica_groups=mesh['dp'=96,'outer'=8] {'outer'}, dimensions={0} | all-to-all | bytes 65536 | tf_op jit(solution)/shard_map/all_to_all | solution.py:218
  86.4 0.0 copy-done.2
  86.4 0.0 copy-done.5
  86.4 1.0 %shard_map.89 = (f32[1,2,4096]{2,1,0:T(2,128)}, f32[2,4096]{1,0:T(2,128)}) custom-call(f32[64,128]{1,0:T(8,128)S(1)} %get-tuple-element.15.moment, f32[8,128]{1,0:T(8,128)S(1)} %get-tuple-element.16.kept, f32[8,8,128]{2,1,0:T(8,128)S(1)} %all_to_all.17.packed, bf16[64,192]{1,0:T(8,128)(2,1)S(1)} %copy-done.5, bf16[384,512]{1,0:T(8,128)(2,1)S(1)} %copy-done.2), custom_call_target="tpu_custom_call" | custom-call | tf_op jit(solution)/shard_map/pallas_call | solution.py:207
  (1 shorter events, 0.0 us)
Async XLA Ops:
  0.6 1.4 %copy-start = (bf16[1,1,192,4096]{3,2,1,0:T(8,128)(2,1)S(1)}, bf16[1,1,192,4096]{3,2,1,0:T(8,128)(2,1)}, u32[]{:S(2)}) copy-start(bf16[1,1,192,4096]{3,2,1,0:T(8,128)(2,1)} %grads.1) | copy-start | bytes 4718596
  3.0 5.3 %collective-permute-start = (f32[3,16,64,128]{3,2,1,0:T(8,128)S(1)}, f32[3,16,64,128]{3,2,1,0:T(8,128)S(1)}, u32[]{:S(2)}, u32[]{:S(2)}) collective-permute-start(f32[3,16,64,128]{3,2,1,0:T(8,128)S(1)} %get-tuple-element.11), channel_id=1, source_target_pairs={{0,8},{8,0},{16,24},{24,16},{32,40},{40,32},{48,56},{56,48},{64,72... | collective-permute-start | bytes 4718600 | tf_op jit(solution)/shard_map/ppermute | solution.py:225
  8.6 23.3 %collective-permute-start.1 = (f32[16,64,128]{2,1,0:T(8,128)S(1)}, f32[16,64,128]{2,1,0:T(8,128)S(1)}, u32[]{:S(2)}, u32[]{:S(2)}) collective-permute-start(f32[16,64,128]{2,1,0:T(8,128)S(1)} %get-tuple-element.13), channel_id=1, source_target_pairs={{0,16},{8,184},{16,32},{24,8},{32,48},{40,24},{48,64},{56,40},{64,... | collective-permute-start | bytes 1572872 | tf_op jit(solution)/shard_map/ppermute | solution.py:227
  12.9 21.8 %collective-permute-start.2 = (f32[16,64,128]{2,1,0:T(8,128)S(1)}, f32[16,64,128]{2,1,0:T(8,128)S(1)}, u32[]{:S(2)}, u32[]{:S(2)}) collective-permute-start(f32[16,64,128]{2,1,0:T(8,128)S(1)} %get-tuple-element.14), channel_id=1, source_target_pairs={{0,176},{8,24},{16,0},{24,40},{32,16},{40,56},{48,32},{56,72},{64,... | collective-permute-start | bytes 1572872 | tf_op jit(solution)/shard_map/ppermute | solution.py:228
  34.7 40.5 %copy-start.1 = (bf16[1536,128]{1,0:T(8,128)(2,1)S(1)}, bf16[1536,128]{1,0:T(8,128)(2,1)}, u32[]{:S(2)}) copy-start(bf16[1536,128]{1,0:T(8,128)(2,1)} %constant.11.clone.right) | copy-start | bytes 1179652
  34.7 40.5 %copy-start.3 = (f32[1,2,4096]{2,1,0:T(2,128)S(1)}, f32[1,2,4096]{2,1,0:T(2,128)}, u32[]{:S(2)}) copy-start(f32[1,2,4096]{2,1,0:T(2,128)} %momentum.1) | copy-start | bytes 98308
  34.7 40.5 %copy-start.4 = (bf16[64,192]{1,0:T(8,128)(2,1)S(1)}, bf16[64,192]{1,0:T(8,128)(2,1)}, u32[]{:S(2)}) copy-start(bf16[64,192]{1,0:T(8,128)(2,1)} %constant.10.clone.left) | copy-start | bytes 73732
  34.7 40.5 %copy-start.6 = (s32[2,2]{1,0:T(2,128)S(1)}, s32[2,2]{1,0:T(2,128)}, u32[]{:S(2)}) copy-start(s32[2,2]{1,0:T(2,128)} %corner.1) | copy-start | bytes 52
  34.8 51.6 %copy-start.2 = (bf16[384,512]{1,0:T(8,128)(2,1)S(1)}, bf16[384,512]{1,0:T(8,128)(2,1)}, u32[]{:S(2)}) copy-start(bf16[384,512]{1,0:T(8,128)(2,1)} %constant.13.clone.right_t) | copy-start | bytes 1179652
  34.8 51.6 %copy-start.5 = (bf16[64,192]{1,0:T(8,128)(2,1)S(1)}, bf16[64,192]{1,0:T(8,128)(2,1)}, u32[]{:S(2)}) copy-start(bf16[64,192]{1,0:T(8,128)(2,1)} %constant.12.clone.left_t) | copy-start | bytes 73732

commit v5 on v4

--- a/solution.py
+++ b/solution.py
@@ -32,15 +32,10 @@
     ]
 
 
-def y_groups():
-    return [[device_of(y, z, c) for y in range(NY)] for z in range(NZ) for c in range(2)]
-
-
-def z_groups():
+def far_groups():
     return [
-        [device_of(y, 3 * q + s, c) for q in range(4)]
-        for s in range(3)
-        for y in range(NY)
+        [device_of(y, 4 * q + s, c) for y in range(NY) for q in range(3)]
+        for s in range(4)
         for c in range(2)
     ]
 
@@ -79,14 +74,14 @@
 
 
 def chunk(y, q, kind, core):
-    return pl.multiple_of(((y * NZ + 3 * q + kind) * 2 + core) * 64, 64)
+    return pl.multiple_of(((y * NZ + 4 * q + kind) * 2 + core) * 64, 64)
 
 
 def place():
     me = lax.axis_index("dp")
     core = lax.rem(me, 2)
     z = lax.rem(me // 2, NZ)
-    return core, [lax.rem(z + d, 3) for d in (1 + core, 2 - core, 0)]
+    return core, [lax.rem(z + d, 4) for d in (2, 1 + 2 * core, 3 - 2 * core, 0)]
 
 
 def arrange_kernel(grads, send, square):
@@ -107,16 +102,16 @@
     lax.fori_loop(0, 12, spread, 0)
 
     def deal(i, carry):
-        y, q = i // 4, lax.rem(i, 4)
-        for slot, kind in enumerate((kinds[1], kinds[0], kinds[2])):
+        y, q = i // 3, lax.rem(i, 3)
+        for slot, kind in enumerate((kinds[0], kinds[2], kinds[1], kinds[3])):
             send[slot, i] = square[pl.ds(chunk(y, q, kind, 1 - core), 64), :]
         return carry
 
-    lax.fori_loop(0, 16, deal, 0)
+    lax.fori_loop(0, 12, deal, 0)
 
 
 def arrange(grads):
-    shapes = [(3, 16, 64, 128), (6144, 128)]
+    shapes = [(4, 12, 64, 128), (6144, 128)]
     return pl.pallas_call(
         arrange_kernel,
         out_shape=tuple(jax.ShapeDtypeStruct(s, jnp.float32) for s in shapes),
@@ -126,17 +121,17 @@
     )(grads)
 
 
-def chip_kernel(square, other, first, second, here):
+def chip_kernel(square, other, far, first, second, here):
     core, kinds = place()
 
     def add(i, carry):
-        y, q = i // 4, lax.rem(i, 4)
-        for slot, ref in enumerate((first, second, here)):
+        y, q = i // 3, lax.rem(i, 3)
+        for slot, ref in enumerate((far, first, second, here)):
             mine = square[pl.ds(chunk(y, q, kinds[slot], core), 64), :]
             ref[i] = mine + other[slot, i]
         return carry
 
-    lax.fori_loop(0, 16, add, 0)
+    lax.fori_loop(0, 12, add, 0)
 
 
 def dot(a, b):
@@ -162,7 +157,9 @@
 def kept_kernel(parts, momentum, corner, left, right, moment, kept, copies, square):
     for t in range(32):
         square[pl.ds(t, 2, stride=32), :] = momentum[0, :, t * 128 : (t + 1) * 128]
-    total = (parts[0] + parts[1]) + (parts[2] + parts[3])
+    total = parts[0]
+    for k in range(1, 12):
+        total = total + parts[k]
     value = 0.9 * square[...] + total / N_DP
     moment[...] = value
     mixed = dot_left(left[...], value)
@@ -223,12 +220,11 @@
     tile = (64, 128)
     send, square = arrange(grads)
     other = lax.ppermute(send, "dp", shift(dcore=1))
-    first, second, here = call(chip_kernel, [(16, 64, 128)] * 3, (square, other))
+    far, first, second, here = call(chip_kernel, [(12, 64, 128)] * 4, (square, other))
+    zero = lax.ppermute(far, "dp", shift(dz=2))
     one = lax.ppermute(first, "dp", shift(dz=1))
     two = lax.ppermute(second, "dp", shift(dz=-1))
-    near = exchange(here + one + two, "dp", y_groups())
-    line = near.reshape(NY, 4, 64, 128).sum(axis=0)
-    parts = exchange(line, "dp", z_groups())
+    parts = exchange(here + one + two + zero, "dp", far_groups())
     moment, kept, copies = call(
         kept_kernel,
         [tile, (8, 128), (N_OUTER, 8, 128)],

time: 87.7 us -> 84.3 us (0.961)
  the two profiles are of different devices: /device:TPU:16 before, /device:TPU:8 now
where the time goes in v5:
time: 84.3 us; the launch traced here: 84 us
  blocking collectives  41.4 us (49%)
  starting transfers between devices  20.5 us (24%)
  waiting for transfers between devices  16.7 us (20%)
  Pallas kernels  3.16 us (4%)
  local copies, waits for them, and re-layouts  1.43 us (2%)
    all_to_all x2, blocking collectives, exchange(): lax.all_to_all(value, axis, 0, 0, axis_index_groups=groups, tiled=True)  41.4 us
    ppermute x1, starting transfers between devices, on_device(): two = lax.ppermute(second, 'dp', shift(dz=-1))  12.2 us
    ppermute x1, waiting for transfers between devices, on_device(): two = lax.ppermute(second, 'dp', shift(dz=-1))  9.69 us
    ppermute x1, starting transfers between devices, on_device(): one = lax.ppermute(first, 'dp', shift(dz=1))  4.41 us
    ppermute x1, waiting for transfers between devices, on_device(): other = lax.ppermute(send, 'dp', shift(dcore=1))  3.38 us
    pallas_call x3, Pallas kernels, call(): pl.pallas_call(kernel, out_shape=tuple((jax.ShapeDtypeStruct(s, jnp.float...  2.2 us
    ppermute x1, waiting for transfers between devices, on_device(): one = lax.ppermute(first, 'dp', shift(dz=1))  2 us
    ppermute x1, starting transfers between devices, on_device(): other = lax.ppermute(send, 'dp', shift(dcore=1))  1.92 us
  transfers between devices with their start and end apart: 4, of which 4 were waited for; matrix products, arithmetic and copies ran while one was open for 0% of the time, Pallas kernels for 0%

profile of v5, /device:TPU:8, one launch (start us, length us, event | category | flops | bytes accessed | tf_op | source)
XLA Modules:
  0.0 84.0 jit_solution(16937817742019589039)
XLA Ops:
  0.6 0.0 copy-start
  0.6 1.4 %copy-done = bf16[1,1,192,4096]{3,2,1,0:T(8,128)(2,1)S(1)} copy-done((bf16[1,1,192,4096]{3,2,1,0:T(8,128)(2,1)S(1)}, bf16[1,1,192,4096]{3,2,1,0:T(8,128)(2,1)}, u32[]{:S(2)}) %copy-start) | copy-done | bytes 1572888
  2.0 1.0 %shard_map.86 = (f32[4,12,64,128]{3,2,1,0:T(8,128)S(1)}, f32[6144,128]{1,0:T(8,128)S(1)}) custom-call(bf16[1,1,192,4096]{3,2,1,0:T(8,128)(2,1)S(1)} %copy-done), custom_call_target="tpu_custom_call" | custom-call | tf_op jit(solution)/shard_map/pallas_call | solution.py:115
  3.0 1.9 %collective-permute-start = (f32[4,12,64,128]{3,2,1,0:T(8,128)S(1)}, f32[4,12,64,128]{3,2,1,0:T(8,128)S(1)}, u32[]{:S(2)}, u32[]{:S(2)}) collective-permute-start(f32[4,12,64,128]{3,2,1,0:T(8,128)S(1)} %get-tuple-element.12), channel_id=1, source_target_pairs={{0,8},{8,0},{16,24},{24,16},{32,40},{40,32},{48,56},{56,48},{64,72... | collective-permute-start | bytes 4718600 | tf_op jit(solution)/shard_map/ppermute | solution.py:222
  4.9 3.4 %collective-permute-done.other = f32[4,12,64,128]{3,2,1,0:T(8,128)S(1)} collective-permute-done((f32[4,12,64,128]{3,2,1,0:T(8,128)S(1)}, f32[4,12,64,128]{3,2,1,0:T(8,128)S(1)}, u32[]{:S(2)}, u32[]{:S(2)}) %collective-permute-start) | collective-permute-done | bytes 1572896 | tf_op jit(solution)/shard_map/ppermute | solution.py:222
  8.3 0.3 shard_map.87
  8.6 0.0 copy-start.2
  8.6 0.0 copy-start.3
  8.6 0.0 copy-start.5
  8.6 0.0 copy-start.6
  8.6 4.4 %collective-permute-start.1 = (f32[12,64,128]{2,1,0:T(8,128)S(1)}, f32[12,64,128]{2,1,0:T(8,128)S(1)}, u32[]{:S(2)}, u32[]{:S(2)}) collective-permute-start(f32[12,64,128]{2,1,0:T(8,128)S(1)} %get-tuple-element.14), channel_id=1, source_target_pairs={{0,16},{8,184},{16,32},{24,8},{32,48},{40,24},{48,64},{56,40},{64,... | collective-permute-start | bytes 1179656 | tf_op jit(solution)/shard_map/ppermute | solution.py:225
  13.1 12.2 %collective-permute-start.2 = (f32[12,64,128]{2,1,0:T(8,128)S(1)}, f32[12,64,128]{2,1,0:T(8,128)S(1)}, u32[]{:S(2)}, u32[]{:S(2)}) collective-permute-start(f32[12,64,128]{2,1,0:T(8,128)S(1)} %get-tuple-element.15), channel_id=1, source_target_pairs={{0,176},{8,24},{16,0},{24,40},{32,16},{40,56},{48,32},{56,72},{64,... | collective-permute-start | bytes 1179656 | tf_op jit(solution)/shard_map/ppermute | solution.py:226
  25.3 1.9 %collective-permute-start.3 = (f32[12,64,128]{2,1,0:T(8,128)S(1)}, f32[12,64,128]{2,1,0:T(8,128)S(1)}, u32[]{:S(2)}, u32[]{:S(2)}) collective-permute-start(f32[12,64,128]{2,1,0:T(8,128)S(1)} %get-tuple-element.16), channel_id=1, source_target_pairs={{0,32},{8,168},{16,48},{24,184},{32,64},{40,8},{48,80},{56,24},{64... | collective-permute-start | bytes 1179656 | tf_op jit(solution)/shard_map/ppermute | solution.py:224
  27.2 2.0 %collective-permute-done.1 = f32[12,64,128]{2,1,0:T(8,128)S(1)} collective-permute-done((f32[12,64,128]{2,1,0:T(8,128)S(1)}, f32[12,64,128]{2,1,0:T(8,128)S(1)}, u32[]{:S(2)}, u32[]{:S(2)}) %collective-permute-start.1) | collective-permute-done | bytes 393248 | tf_op jit(solution)/shard_map/ppermute | solution.py:225
  29.2 9.7 %collective-permute-done.2 = f32[12,64,128]{2,1,0:T(8,128)S(1)} collective-permute-done((f32[12,64,128]{2,1,0:T(8,128)S(1)}, f32[12,64,128]{2,1,0:T(8,128)S(1)}, u32[]{:S(2)}, u32[]{:S(2)}) %collective-permute-start.2) | collective-permute-done | bytes 393248 | tf_op jit(solution)/shard_map/ppermute | solution.py:226
  38.9 1.6 %collective-permute-done.3 = f32[12,64,128]{2,1,0:T(8,128)S(1)} collective-permute-done((f32[12,64,128]{2,1,0:T(8,128)S(1)}, f32[12,64,128]{2,1,0:T(8,128)S(1)}, u32[]{:S(2)}, u32[]{:S(2)}) %collective-permute-start.3) | collective-permute-done | bytes 393248 | tf_op jit(solution)/shard_map/ppermute | solution.py:224
  40.5 0.0 copy-start.1
  40.5 0.0 copy-start.4
  40.5 0.1 add_add_fusion
  40.6 30.9 %all_to_all.10.parts = f32[12,64,128]{2,1,0:T(8,128)S(1)} all-to-all(f32[12,64,128]{2,1,0:T(8,128)S(1)} %add_add_fusion), channel_id=1, replica_groups={{0,64,128,192,256,320,384,448,512,576,640,704},{8,72,136,200,264,328,39..., dimensions={0} | all-to-all | bytes 786432 | tf_op jit(solution)/shard_map/all_to_all | solution.py:215
  71.5 0.0 copy-done.2
  71.5 0.0 copy-done.3
  71.5 0.0 copy-done.5
  71.5 0.0 copy-done.6
  71.5 0.9 %shard_map.88 = (f32[64,128]{1,0:T(8,128)S(1)}, f32[8,128]{1,0:T(8,128)S(1)}, f32[8,8,128]{2,1,0:T(8,128)S(1)}) custom-call(f32[12,64,128]{2,1,0:T(8,128)S(1)} %all_to_all.10.parts, f32[1,2,4096]{2,1,0:T(2,128)S(1)} %copy-done.3, s32[2,2]{1,0:T(2,128)S(1)} %copy-done.6, bf16[64,192]{1,0:T(8,128)(2,1)S(1)} %copy-done.5, bf16[1536,128]{1,0:T(8,128)(2,1)S(1)} %copy-done.2), custom_call_target="tpu_custom_call" | custom-call | tf_op jit(solution)/shard_map/pallas_call | solution.py:204
  72.4 10.5 %all_to_all.11.packed = f32[8,8,128]{2,1,0:T(8,128)S(1)} all-to-all(f32[8,8,128]{2,1,0:T(8,128)S(1)} %get-tuple-element.19), channel_id=1, replica_groups=mesh['dp'=96,'outer'=8] {'outer'}, dimensions={0} | all-to-all | bytes 65536 | tf_op jit(solution)/shard_map/all_to_all | solution.py:215
  82.9 0.0 copy-done.1
  82.9 0.0 copy-done.4
  82.9 1.0 %shard_map.89 = (f32[1,2,4096]{2,1,0:T(2,128)}, f32[2,4096]{1,0:T(2,128)}) custom-call(f32[64,128]{1,0:T(8,128)S(1)} %get-tuple-element.17.moment, f32[8,128]{1,0:T(8,128)S(1)} %get-tuple-element.18.kept, f32[8,8,128]{2,1,0:T(8,128)S(1)} %all_to_all.11.packed, bf16[64,192]{1,0:T(8,128)(2,1)S(1)} %copy-done.4, bf16[384,512]{1,0:T(8,128)(2,1)S(1)} %copy-done.1), custom_call_target="tpu_custom_call" | custom-call | tf_op jit(solution)/shard_map/pallas_call | solution.py:204
Async XLA Ops:
  0.6 1.4 %copy-start = (bf16[1,1,192,4096]{3,2,1,0:T(8,128)(2,1)S(1)}, bf16[1,1,192,4096]{3,2,1,0:T(8,128)(2,1)}, u32[]{:S(2)}) copy-start(bf16[1,1,192,4096]{3,2,1,0:T(8,128)(2,1)} %grads.1) | copy-start | bytes 4718596
  3.0 5.3 %collective-permute-start = (f32[4,12,64,128]{3,2,1,0:T(8,128)S(1)}, f32[4,12,64,128]{3,2,1,0:T(8,128)S(1)}, u32[]{:S(2)}, u32[]{:S(2)}) collective-permute-start(f32[4,12,64,128]{3,2,1,0:T(8,128)S(1)} %get-tuple-element.12), channel_id=1, source_target_pairs={{0,8},{8,0},{16,24},{24,16},{32,40},{40,32},{48,56},{56,48},{64,72... | collective-permute-start | bytes 4718600 | tf_op jit(solution)/shard_map/ppermute | solution.py:222
  8.6 62.9 %copy-start.2 = (bf16[1536,128]{1,0:T(8,128)(2,1)S(1)}, bf16[1536,128]{1,0:T(8,128)(2,1)}, u32[]{:S(2)}) copy-start(bf16[1536,128]{1,0:T(8,128)(2,1)} %constant.9.clone.right) | copy-start | bytes 1179652
  8.6 62.9 %copy-start.3 = (f32[1,2,4096]{2,1,0:T(2,128)S(1)}, f32[1,2,4096]{2,1,0:T(2,128)}, u32[]{:S(2)}) copy-start(f32[1,2,4096]{2,1,0:T(2,128)} %momentum.1) | copy-start | bytes 98308
  8.6 62.9 %copy-start.5 = (bf16[64,192]{1,0:T(8,128)(2,1)S(1)}, bf16[64,192]{1,0:T(8,128)(2,1)}, u32[]{:S(2)}) copy-start(bf16[64,192]{1,0:T(8,128)(2,1)} %constant.8.clone.left) | copy-start | bytes 73732
  8.6 62.9 %copy-start.6 = (s32[2,2]{1,0:T(2,128)S(1)}, s32[2,2]{1,0:T(2,128)}, u32[]{:S(2)}) copy-start(s32[2,2]{1,0:T(2,128)} %corner.1) | copy-start | bytes 52
  8.6 20.6 %collective-permute-start.1 = (f32[12,64,128]{2,1,0:T(8,128)S(1)}, f32[12,64,128]{2,1,0:T(8,128)S(1)}, u32[]{:S(2)}, u32[]{:S(2)}) collective-permute-start(f32[12,64,128]{2,1,0:T(8,128)S(1)} %get-tuple-element.14), channel_id=1, source_target_pairs={{0,16},{8,184},{16,32},{24,8},{32,48},{40,24},{48,64},{56,40},{64,... | collective-permute-start | bytes 1179656 | tf_op jit(solution)/shard_map/ppermute | solution.py:225
  13.1 25.9 %collective-permute-start.2 = (f32[12,64,128]{2,1,0:T(8,128)S(1)}, f32[12,64,128]{2,1,0:T(8,128)S(1)}, u32[]{:S(2)}, u32[]{:S(2)}) collective-permute-start(f32[12,64,128]{2,1,0:T(8,128)S(1)} %get-tuple-element.15), channel_id=1, source_target_pairs={{0,176},{8,24},{16,0},{24,40},{32,16},{40,56},{48,32},{56,72},{64,... | collective-permute-start | bytes 1179656 | tf_op jit(solution)/shard_map/ppermute | solution.py:226
  25.3 15.2 %collective-permute-start.3 = (f32[12,64,128]{2,1,0:T(8,128)S(1)}, f32[12,64,128]{2,1,0:T(8,128)S(1)}, u32[]{:S(2)}, u32[]{:S(2)}) collective-permute-start(f32[12,64,128]{2,1,0:T(8,128)S(1)} %get-tuple-element.16), channel_id=1, source_target_pairs={{0,32},{8,168},{16,48},{24,184},{32,64},{40,8},{48,80},{56,24},{64... | collective-permute-start | bytes 1179656 | tf_op jit(solution)/shard_map/ppermute | solution.py:224
  40.5 42.4 %copy-start.1 = (bf16[384,512]{1,0:T(8,128)(2,1)S(1)}, bf16[384,512]{1,0:T(8,128)(2,1)}, u32[]{:S(2)}) copy-start(bf16[384,512]{1,0:T(8,128)(2,1)} %constant.11.clone.right_t) | copy-start | bytes 1179652
  40.5 42.4 %copy-start.4 = (bf16[64,192]{1,0:T(8,128)(2,1)S(1)}, bf16[64,192]{1,0:T(8,128)(2,1)}, u32[]{:S(2)}) copy-start(bf16[64,192]{1,0:T(8,128)(2,1)} %constant.10.clone.left_t) | copy-start | bytes 73732

commit v6 on v5

--- a/solution.py
+++ b/solution.py
@@ -34,7 +34,7 @@
 
 def far_groups():
     return [
-        [device_of(y, 4 * q + s, c) for y in range(NY) for q in range(3)]
+        [device_of(y, 4 * q + s, c) for y in range(NY) for q in range(3)][:: 1 - 2 * c]
         for s in range(4)
         for c in range(2)
     ]
@@ -77,6 +77,11 @@
     return pl.multiple_of(((y * NZ + 4 * q + kind) * 2 + core) * 64, 64)
 
 
+def member(i, core):
+    i = i + core * (11 - 2 * i)
+    return i // 3, lax.rem(i, 3)
+
+
 def place():
     me = lax.axis_index("dp")
     core = lax.rem(me, 2)
@@ -102,7 +107,7 @@
     lax.fori_loop(0, 12, spread, 0)
 
     def deal(i, carry):
-        y, q = i // 3, lax.rem(i, 3)
+        y, q = member(i, 1 - core)
         for slot, kind in enumerate((kinds[0], kinds[2], kinds[1], kinds[3])):
             send[slot, i] = square[pl.ds(chunk(y, q, kind, 1 - core), 64), :]
         return carry
@@ -125,7 +130,7 @@
     core, kinds = place()
 
     def add(i, carry):
-        y, q = i // 3, lax.rem(i, 3)
+        y, q = member(i, core)
         for slot, ref in enumerate((far, first, second, here)):
             mine = square[pl.ds(chunk(y, q, kinds[slot], core), 64), :]
             ref[i] = mine + other[slot, i]

time: 84.3 us -> 81.8 us (0.970)
  the two profiles are of different devices: /device:TPU:8 before, /device:TPU:64 now
where the time goes in v6:
time: 81.8 us; the launch traced here: 81.4 us
  blocking collectives  38.5 us (47%)
  waiting for transfers between devices  21 us (26%)
  starting transfers between devices  16.5 us (20%)
  Pallas kernels  3.22 us (4%)
  local copies, waits for them, and re-layouts  1.43 us (2%)
    all_to_all x2, blocking collectives, exchange(): lax.all_to_all(value, axis, 0, 0, axis_index_groups=groups, tiled=True)  38.5 us
    ppermute x1, waiting for transfers between devices, on_device(): zero = lax.ppermute(far, 'dp', shift(dz=2))  12.7 us
    ppermute x1, starting transfers between devices, on_device(): two = lax.ppermute(second, 'dp', shift(dz=-1))  8.21 us
    ppermute x1, starting transfers between devices, on_device(): one = lax.ppermute(first, 'dp', shift(dz=1))  4.41 us
    ppermute x1, waiting for transfers between devices, on_device(): other = lax.ppermute(send, 'dp', shift(dcore=1))  3.38 us
    ppermute x1, waiting for transfers between devices, on_device(): two = lax.ppermute(second, 'dp', shift(dz=-1))  3.05 us
    pallas_call x3, Pallas kernels, call(): pl.pallas_call(kernel, out_shape=tuple((jax.ShapeDtypeStruct(s, jnp.float...  2.23 us
    ppermute x1, starting transfers between devices, on_device(): other = lax.ppermute(send, 'dp', shift(dcore=1))  1.92 us
  transfers between devices with their start and end apart: 4, of which 4 were waited for; matrix products, arithmetic and copies ran while one was open for 0% of the time, Pallas kernels for 0%

profile of v6, /device:TPU:64, one launch (start us, length us, event | category | flops | bytes accessed | tf_op | source)
XLA Modules:
  0.0 81.4 jit_solution(14509113256631853225)
XLA Ops:
  0.6 0.0 copy-start
  0.6 1.4 %copy-done = bf16[1,1,192,4096]{3,2,1,0:T(8,128)(2,1)S(1)} copy-done((bf16[1,1,192,4096]{3,2,1,0:T(8,128)(2,1)S(1)}, bf16[1,1,192,4096]{3,2,1,0:T(8,128)(2,1)}, u32[]{:S(2)}) %copy-start) | copy-done | bytes 1572888
  2.0 1.0 %shard_map.86 = (f32[4,12,64,128]{3,2,1,0:T(8,128)S(1)}, f32[6144,128]{1,0:T(8,128)S(1)}) custom-call(bf16[1,1,192,4096]{3,2,1,0:T(8,128)(2,1)S(1)} %copy-done), custom_call_target="tpu_custom_call" | custom-call | tf_op jit(solution)/shard_map/pallas_call | solution.py:120
  3.0 1.9 %collective-permute-start = (f32[4,12,64,128]{3,2,1,0:T(8,128)S(1)}, f32[4,12,64,128]{3,2,1,0:T(8,128)S(1)}, u32[]{:S(2)}, u32[]{:S(2)}) collective-permute-start(f32[4,12,64,128]{3,2,1,0:T(8,128)S(1)} %get-tuple-element.12), channel_id=1, source_target_pairs={{0,8},{8,0},{16,24},{24,16},{32,40},{40,32},{48,56},{56,48},{64,72... | collective-permute-start | bytes 4718600 | tf_op jit(solution)/shard_map/ppermute | solution.py:227
  5.0 3.4 %collective-permute-done.other = f32[4,12,64,128]{3,2,1,0:T(8,128)S(1)} collective-permute-done((f32[4,12,64,128]{3,2,1,0:T(8,128)S(1)}, f32[4,12,64,128]{3,2,1,0:T(8,128)S(1)}, u32[]{:S(2)}, u32[]{:S(2)}) %collective-permute-start) | collective-permute-done | bytes 1572896 | tf_op jit(solution)/shard_map/ppermute | solution.py:227
  8.3 0.3 shard_map.87
  8.7 0.0 copy-start.2
  8.7 0.0 copy-start.3
  8.7 0.0 copy-start.5
  8.7 0.0 copy-start.6
  8.7 4.4 %collective-permute-start.1 = (f32[12,64,128]{2,1,0:T(8,128)S(1)}, f32[12,64,128]{2,1,0:T(8,128)S(1)}, u32[]{:S(2)}, u32[]{:S(2)}) collective-permute-start(f32[12,64,128]{2,1,0:T(8,128)S(1)} %get-tuple-element.14), channel_id=1, source_target_pairs={{0,16},{8,184},{16,32},{24,8},{32,48},{40,24},{48,64},{56,40},{64,... | collective-permute-start | bytes 1179656 | tf_op jit(solution)/shard_map/ppermute | solution.py:230
  13.1 8.2 %collective-permute-start.2 = (f32[12,64,128]{2,1,0:T(8,128)S(1)}, f32[12,64,128]{2,1,0:T(8,128)S(1)}, u32[]{:S(2)}, u32[]{:S(2)}) collective-permute-start(f32[12,64,128]{2,1,0:T(8,128)S(1)} %get-tuple-element.15), channel_id=1, source_target_pairs={{0,176},{8,24},{16,0},{24,40},{32,16},{40,56},{48,32},{56,72},{64,... | collective-permute-start | bytes 1179656 | tf_op jit(solution)/shard_map/ppermute | solution.py:231
  21.4 1.9 %collective-permute-start.3 = (f32[12,64,128]{2,1,0:T(8,128)S(1)}, f32[12,64,128]{2,1,0:T(8,128)S(1)}, u32[]{:S(2)}, u32[]{:S(2)}) collective-permute-start(f32[12,64,128]{2,1,0:T(8,128)S(1)} %get-tuple-element.16), channel_id=1, source_target_pairs={{0,32},{8,168},{16,48},{24,184},{32,64},{40,8},{48,80},{56,24},{64... | collective-permute-start | bytes 1179656 | tf_op jit(solution)/shard_map/ppermute | solution.py:229
  23.3 1.9 %collective-permute-done.1 = f32[12,64,128]{2,1,0:T(8,128)S(1)} collective-permute-done((f32[12,64,128]{2,1,0:T(8,128)S(1)}, f32[12,64,128]{2,1,0:T(8,128)S(1)}, u32[]{:S(2)}, u32[]{:S(2)}) %collective-permute-start.1) | collective-permute-done | bytes 393248 | tf_op jit(solution)/shard_map/ppermute | solution.py:230
  25.2 3.0 %collective-permute-done.2 = f32[12,64,128]{2,1,0:T(8,128)S(1)} collective-permute-done((f32[12,64,128]{2,1,0:T(8,128)S(1)}, f32[12,64,128]{2,1,0:T(8,128)S(1)}, u32[]{:S(2)}, u32[]{:S(2)}) %collective-permute-start.2) | collective-permute-done | bytes 393248 | tf_op jit(solution)/shard_map/ppermute | solution.py:231
  28.2 12.7 %collective-permute-done.3 = f32[12,64,128]{2,1,0:T(8,128)S(1)} collective-permute-done((f32[12,64,128]{2,1,0:T(8,128)S(1)}, f32[12,64,128]{2,1,0:T(8,128)S(1)}, u32[]{:S(2)}, u32[]{:S(2)}) %collective-permute-start.3) | collective-permute-done | bytes 393248 | tf_op jit(solution)/shard_map/ppermute | solution.py:229
  40.9 0.0 copy-start.1
  40.9 0.0 copy-start.4
  40.9 0.1 add_add_fusion
  41.0 27.2 %all_to_all.10.parts = f32[12,64,128]{2,1,0:T(8,128)S(1)} all-to-all(f32[12,64,128]{2,1,0:T(8,128)S(1)} %add_add_fusion), channel_id=1, replica_groups={{0,64,128,192,256,320,384,448,512,576,640,704},{712,648,584,520,456,392..., dimensions={0} | all-to-all | bytes 786432 | tf_op jit(solution)/shard_map/all_to_all | solution.py:220
  68.2 0.0 copy-done.2
  68.2 0.0 copy-done.3
  68.2 0.0 copy-done.5
  68.2 0.0 copy-done.6
  68.2 0.9 %shard_map.88 = (f32[64,128]{1,0:T(8,128)S(1)}, f32[8,128]{1,0:T(8,128)S(1)}, f32[8,8,128]{2,1,0:T(8,128)S(1)}) custom-call(f32[12,64,128]{2,1,0:T(8,128)S(1)} %all_to_all.10.parts, f32[1,2,4096]{2,1,0:T(2,128)S(1)} %copy-done.3, s32[2,2]{1,0:T(2,128)S(1)} %copy-done.6, bf16[64,192]{1,0:T(8,128)(2,1)S(1)} %copy-done.5, bf16[1536,128]{1,0:T(8,128)(2,1)S(1)} %copy-done.2), custom_call_target="tpu_custom_call" | custom-call | tf_op jit(solution)/shard_map/pallas_call | solution.py:209
  69.1 11.3 %all_to_all.11.packed = f32[8,8,128]{2,1,0:T(8,128)S(1)} all-to-all(f32[8,8,128]{2,1,0:T(8,128)S(1)} %get-tuple-element.19), channel_id=1, replica_groups=mesh['dp'=96,'outer'=8] {'outer'}, dimensions={0} | all-to-all | bytes 65536 | tf_op jit(solution)/shard_map/all_to_all | solution.py:220
  80.4 0.0 copy-done.1
  80.4 0.0 copy-done.4
  80.4 1.0 %shard_map.89 = (f32[1,2,4096]{2,1,0:T(2,128)}, f32[2,4096]{1,0:T(2,128)}) custom-call(f32[64,128]{1,0:T(8,128)S(1)} %get-tuple-element.17.moment, f32[8,128]{1,0:T(8,128)S(1)} %get-tuple-element.18.kept, f32[8,8,128]{2,1,0:T(8,128)S(1)} %all_to_all.11.packed, bf16[64,192]{1,0:T(8,128)(2,1)S(1)} %copy-done.4, bf16[384,512]{1,0:T(8,128)(2,1)S(1)} %copy-done.1), custom_call_target="tpu_custom_call" | custom-call | tf_op jit(solution)/shard_map/pallas_call | solution.py:209
Async XLA Ops:
  0.6 1.4 %copy-start = (bf16[1,1,192,4096]{3,2,1,0:T(8,128)(2,1)S(1)}, bf16[1,1,192,4096]{3,2,1,0:T(8,128)(2,1)}, u32[]{:S(2)}) copy-start(bf16[1,1,192,4096]{3,2,1,0:T(8,128)(2,1)} %grads.1) | copy-start | bytes 4718596
  3.0 5.3 %collective-permute-start = (f32[4,12,64,128]{3,2,1,0:T(8,128)S(1)}, f32[4,12,64,128]{3,2,1,0:T(8,128)S(1)}, u32[]{:S(2)}, u32[]{:S(2)}) collective-permute-start(f32[4,12,64,128]{3,2,1,0:T(8,128)S(1)} %get-tuple-element.12), channel_id=1, source_target_pairs={{0,8},{8,0},{16,24},{24,16},{32,40},{40,32},{48,56},{56,48},{64,72... | collective-permute-start | bytes 4718600 | tf_op jit(solution)/shard_map/ppermute | solution.py:227
  8.7 59.5 %copy-start.2 = (bf16[1536,128]{1,0:T(8,128)(2,1)S(1)}, bf16[1536,128]{1,0:T(8,128)(2,1)}, u32[]{:S(2)}) copy-start(bf16[1536,128]{1,0:T(8,128)(2,1)} %constant.9.clone.right) | copy-start | bytes 1179652
  8.7 59.5 %copy-start.3 = (f32[1,2,4096]{2,1,0:T(2,128)S(1)}, f32[1,2,4096]{2,1,0:T(2,128)}, u32[]{:S(2)}) copy-start(f32[1,2,4096]{2,1,0:T(2,128)} %momentum.1) | copy-start | bytes 98308
  8.7 59.5 %copy-start.5 = (bf16[64,192]{1,0:T(8,128)(2,1)S(1)}, bf16[64,192]{1,0:T(8,128)(2,1)}, u32[]{:S(2)}) copy-start(bf16[64,192]{1,0:T(8,128)(2,1)} %constant.8.clone.left) | copy-start | bytes 73732
  8.7 59.5 %copy-start.6 = (s32[2,2]{1,0:T(2,128)S(1)}, s32[2,2]{1,0:T(2,128)}, u32[]{:S(2)}) copy-start(s32[2,2]{1,0:T(2,128)} %corner.1) | copy-start | bytes 52
  8.7 16.5 %collective-permute-start.1 = (f32[12,64,128]{2,1,0:T(8,128)S(1)}, f32[12,64,128]{2,1,0:T(8,128)S(1)}, u32[]{:S(2)}, u32[]{:S(2)}) collective-permute-start(f32[12,64,128]{2,1,0:T(8,128)S(1)} %get-tuple-element.14), channel_id=1, source_target_pairs={{0,16},{8,184},{16,32},{24,8},{32,48},{40,24},{48,64},{56,40},{64,... | collective-permute-start | bytes 1179656 | tf_op jit(solution)/shard_map/ppermute | solution.py:230
  13.1 15.1 %collective-permute-start.2 = (f32[12,64,128]{2,1,0:T(8,128)S(1)}, f32[12,64,128]{2,1,0:T(8,128)S(1)}, u32[]{:S(2)}, u32[]{:S(2)}) collective-permute-start(f32[12,64,128]{2,1,0:T(8,128)S(1)} %get-tuple-element.15), channel_id=1, source_target_pairs={{0,176},{8,24},{16,0},{24,40},{32,16},{40,56},{48,32},{56,72},{64,... | collective-permute-start | bytes 1179656 | tf_op jit(solution)/shard_map/ppermute | solution.py:231
  21.4 19.6 %collective-permute-start.3 = (f32[12,64,128]{2,1,0:T(8,128)S(1)}, f32[12,64,128]{2,1,0:T(8,128)S(1)}, u32[]{:S(2)}, u32[]{:S(2)}) collective-permute-start(f32[12,64,128]{2,1,0:T(8,128)S(1)} %get-tuple-element.16), channel_id=1, source_target_pairs={{0,32},{8,168},{16,48},{24,184},{32,64},{40,8},{48,80},{56,24},{64... | collective-permute-start | bytes 1179656 | tf_op jit(solution)/shard_map/ppermute | solution.py:229
  40.9 39.5 %copy-start.1 = (bf16[384,512]{1,0:T(8,128)(2,1)S(1)}, bf16[384,512]{1,0:T(8,128)(2,1)}, u32[]{:S(2)}) copy-start(bf16[384,512]{1,0:T(8,128)(2,1)} %constant.11.clone.right_t) | copy-start | bytes 1179652
  40.9 39.5 %copy-start.4 = (bf16[64,192]{1,0:T(8,128)(2,1)S(1)}, bf16[64,192]{1,0:T(8,128)(2,1)}, u32[]{:S(2)}) copy-start(bf16[64,192]{1,0:T(8,128)(2,1)} %constant.10.clone.left_t) | copy-start | bytes 73732

commit v7 on v6

--- a/solution.py
+++ b/solution.py
@@ -32,9 +32,14 @@
     ]
 
 
+def far_order(core):
+    by_z = [(y, q) for q in range(3) for y in range(NY)]
+    return by_z[::-1] if core else by_z
+
+
 def far_groups():
     return [
-        [device_of(y, 4 * q + s, c) for y in range(NY) for q in range(3)][:: 1 - 2 * c]
+        [device_of(y, 4 * q + s, c) for y, q in far_order(c)]
         for s in range(4)
         for c in range(2)
     ]
@@ -79,7 +84,7 @@
 
 def member(i, core):
     i = i + core * (11 - 2 * i)
-    return i // 3, lax.rem(i, 3)
+    return lax.rem(i, 4), i // 4
 
 
 def place():

time: 81.8 us -> 81.2 us (level)
  the two profiles are of different devices: /device:TPU:64 before, /device:TPU:48 now
where the time goes in v7:
time: 81.2 us; the launch traced here: 80.8 us
  blocking collectives  38.3 us (47%)
  starting transfers between devices  20.5 us (25%)
  waiting for transfers between devices  16.7 us (21%)
  Pallas kernels  3.11 us (4%)
  local copies, waits for them, and re-layouts  1.43 us (2%)
    all_to_all x2, blocking collectives, exchange(): lax.all_to_all(value, axis, 0, 0, axis_index_groups=groups, tiled=True)  38.3 us
    ppermute x1, starting transfers between devices, on_device(): two = lax.ppermute(second, 'dp', shift(dz=-1))  12.2 us
    ppermute x1, waiting for transfers between devices, on_device(): two = lax.ppermute(second, 'dp', shift(dz=-1))  9.69 us
    ppermute x1, starting transfers between devices, on_device(): one = lax.ppermute(first, 'dp', shift(dz=1))  4.41 us
    ppermute x1, waiting for transfers between devices, on_device(): other = lax.ppermute(send, 'dp', shift(dcore=1))  3.38 us
    pallas_call x3, Pallas kernels, call(): pl.pallas_call(kernel, out_shape=tuple((jax.ShapeDtypeStruct(s, jnp.float...  2.18 us
    ppermute x1, waiting for transfers between devices, on_device(): one = lax.ppermute(first, 'dp', shift(dz=1))  2 us
    ppermute x1, starting transfers between devices, on_device(): other = lax.ppermute(send, 'dp', shift(dcore=1))  1.92 us
  transfers between devices with their start and end apart: 4, of which 4 were waited for; matrix products, arithmetic and copies ran while one was open for 0% of the time, Pallas kernels for 0%

profile of v7, /device:TPU:48, one launch (start us, length us, event | category | flops | bytes accessed | tf_op | source)
XLA Modules:
  0.0 80.8 jit_solution(14714869679277689967)
XLA Ops:
  0.6 0.0 copy-start
  0.6 1.4 %copy-done = bf16[1,1,192,4096]{3,2,1,0:T(8,128)(2,1)S(1)} copy-done((bf16[1,1,192,4096]{3,2,1,0:T(8,128)(2,1)S(1)}, bf16[1,1,192,4096]{3,2,1,0:T(8,128)(2,1)}, u32[]{:S(2)}) %copy-start) | copy-done | bytes 1572888
  2.0 0.9 %shard_map.86 = (f32[4,12,64,128]{3,2,1,0:T(8,128)S(1)}, f32[6144,128]{1,0:T(8,128)S(1)}) custom-call(bf16[1,1,192,4096]{3,2,1,0:T(8,128)(2,1)S(1)} %copy-done), custom_call_target="tpu_custom_call" | custom-call | tf_op jit(solution)/shard_map/pallas_call | solution.py:125
  3.0 1.9 %collective-permute-start = (f32[4,12,64,128]{3,2,1,0:T(8,128)S(1)}, f32[4,12,64,128]{3,2,1,0:T(8,128)S(1)}, u32[]{:S(2)}, u32[]{:S(2)}) collective-permute-start(f32[4,12,64,128]{3,2,1,0:T(8,128)S(1)} %get-tuple-element.12), channel_id=1, source_target_pairs={{0,8},{8,0},{16,24},{24,16},{32,40},{40,32},{48,56},{56,48},{64,72... | collective-permute-start | bytes 4718600 | tf_op jit(solution)/shard_map/ppermute | solution.py:232
  4.9 3.4 %collective-permute-done.other = f32[4,12,64,128]{3,2,1,0:T(8,128)S(1)} collective-permute-done((f32[4,12,64,128]{3,2,1,0:T(8,128)S(1)}, f32[4,12,64,128]{3,2,1,0:T(8,128)S(1)}, u32[]{:S(2)}, u32[]{:S(2)}) %collective-permute-start) | collective-permute-done | bytes 1572896 | tf_op jit(solution)/shard_map/ppermute | solution.py:232
  8.3 0.3 shard_map.87
  8.6 0.0 copy-start.2
  8.6 0.0 copy-start.3
  8.6 0.0 copy-start.5
  8.6 0.0 copy-start.6
  8.6 4.4 %collective-permute-start.1 = (f32[12,64,128]{2,1,0:T(8,128)S(1)}, f32[12,64,128]{2,1,0:T(8,128)S(1)}, u32[]{:S(2)}, u32[]{:S(2)}) collective-permute-start(f32[12,64,128]{2,1,0:T(8,128)S(1)} %get-tuple-element.14), channel_id=1, source_target_pairs={{0,16},{8,184},{16,32},{24,8},{32,48},{40,24},{48,64},{56,40},{64,... | collective-permute-start | bytes 1179656 | tf_op jit(solution)/shard_map/ppermute | solution.py:235
  13.0 12.2 %collective-permute-start.2 = (f32[12,64,128]{2,1,0:T(8,128)S(1)}, f32[12,64,128]{2,1,0:T(8,128)S(1)}, u32[]{:S(2)}, u32[]{:S(2)}) collective-permute-start(f32[12,64,128]{2,1,0:T(8,128)S(1)} %get-tuple-element.15), channel_id=1, source_target_pairs={{0,176},{8,24},{16,0},{24,40},{32,16},{40,56},{48,32},{56,72},{64,... | collective-permute-start | bytes 1179656 | tf_op jit(solution)/shard_map/ppermute | solution.py:236
  25.3 1.9 %collective-permute-start.3 = (f32[12,64,128]{2,1,0:T(8,128)S(1)}, f32[12,64,128]{2,1,0:T(8,128)S(1)}, u32[]{:S(2)}, u32[]{:S(2)}) collective-permute-start(f32[12,64,128]{2,1,0:T(8,128)S(1)} %get-tuple-element.16), channel_id=1, source_target_pairs={{0,32},{8,168},{16,48},{24,184},{32,64},{40,8},{48,80},{56,24},{64... | collective-permute-start | bytes 1179656 | tf_op jit(solution)/shard_map/ppermute | solution.py:234
  27.2 2.0 %collective-permute-done.1 = f32[12,64,128]{2,1,0:T(8,128)S(1)} collective-permute-done((f32[12,64,128]{2,1,0:T(8,128)S(1)}, f32[12,64,128]{2,1,0:T(8,128)S(1)}, u32[]{:S(2)}, u32[]{:S(2)}) %collective-permute-start.1) | collective-permute-done | bytes 393248 | tf_op jit(solution)/shard_map/ppermute | solution.py:235
  29.2 9.7 %collective-permute-done.2 = f32[12,64,128]{2,1,0:T(8,128)S(1)} collective-permute-done((f32[12,64,128]{2,1,0:T(8,128)S(1)}, f32[12,64,128]{2,1,0:T(8,128)S(1)}, u32[]{:S(2)}, u32[]{:S(2)}) %collective-permute-start.2) | collective-permute-done | bytes 393248 | tf_op jit(solution)/shard_map/ppermute | solution.py:236
  38.9 1.6 %collective-permute-done.3 = f32[12,64,128]{2,1,0:T(8,128)S(1)} collective-permute-done((f32[12,64,128]{2,1,0:T(8,128)S(1)}, f32[12,64,128]{2,1,0:T(8,128)S(1)}, u32[]{:S(2)}, u32[]{:S(2)}) %collective-permute-start.3) | collective-permute-done | bytes 393248 | tf_op jit(solution)/shard_map/ppermute | solution.py:234
  40.5 0.0 copy-start.1
  40.5 0.0 copy-start.4
  40.5 0.1 add_add_fusion
  40.6 27.1 %all_to_all.10.parts = f32[12,64,128]{2,1,0:T(8,128)S(1)} all-to-all(f32[12,64,128]{2,1,0:T(8,128)S(1)} %add_add_fusion), channel_id=1, replica_groups={{0,192,384,576,64,256,448,640,128,320,512,704},{712,520,328,136,648,456..., dimensions={0} | all-to-all | bytes 786432 | tf_op jit(solution)/shard_map/all_to_all | solution.py:225
  67.7 0.0 copy-done.2
  67.7 0.0 copy-done.3
  67.7 0.0 copy-done.5
  67.8 0.0 copy-done.6
  67.8 0.9 %shard_map.88 = (f32[64,128]{1,0:T(8,128)S(1)}, f32[8,128]{1,0:T(8,128)S(1)}, f32[8,8,128]{2,1,0:T(8,128)S(1)}) custom-call(f32[12,64,128]{2,1,0:T(8,128)S(1)} %all_to_all.10.parts, f32[1,2,4096]{2,1,0:T(2,128)S(1)} %copy-done.3, s32[2,2]{1,0:T(2,128)S(1)} %copy-done.6, bf16[64,192]{1,0:T(8,128)(2,1)S(1)} %copy-done.5, bf16[1536,128]{1,0:T(8,128)(2,1)S(1)} %copy-done.2), custom_call_target="tpu_custom_call" | custom-call | tf_op jit(solution)/shard_map/pallas_call | solution.py:214
  68.7 11.2 %all_to_all.11.packed = f32[8,8,128]{2,1,0:T(8,128)S(1)} all-to-all(f32[8,8,128]{2,1,0:T(8,128)S(1)} %get-tuple-element.19), channel_id=1, replica_groups=mesh['dp'=96,'outer'=8] {'outer'}, dimensions={0} | all-to-all | bytes 65536 | tf_op jit(solution)/shard_map/all_to_all | solution.py:225
  79.8 0.0 copy-done.1
  79.8 0.0 copy-done.4
  79.8 1.0 %shard_map.89 = (f32[1,2,4096]{2,1,0:T(2,128)}, f32[2,4096]{1,0:T(2,128)}) custom-call(f32[64,128]{1,0:T(8,128)S(1)} %get-tuple-element.17.moment, f32[8,128]{1,0:T(8,128)S(1)} %get-tuple-element.18.kept, f32[8,8,128]{2,1,0:T(8,128)S(1)} %all_to_all.11.packed, bf16[64,192]{1,0:T(8,128)(2,1)S(1)} %copy-done.4, bf16[384,512]{1,0:T(8,128)(2,1)S(1)} %copy-done.1), custom_call_target="tpu_custom_call" | custom-call | tf_op jit(solution)/shard_map/pallas_call | solution.py:214
Async XLA Ops:
  0.6 1.4 %copy-start = (bf16[1,1,192,4096]{3,2,1,0:T(8,128)(2,1)S(1)}, bf16[1,1,192,4096]{3,2,1,0:T(8,128)(2,1)}, u32[]{:S(2)}) copy-start(bf16[1,1,192,4096]{3,2,1,0:T(8,128)(2,1)} %grads.1) | copy-start | bytes 4718596
  3.0 5.3 %collective-permute-start = (f32[4,12,64,128]{3,2,1,0:T(8,128)S(1)}, f32[4,12,64,128]{3,2,1,0:T(8,128)S(1)}, u32[]{:S(2)}, u32[]{:S(2)}) collective-permute-start(f32[4,12,64,128]{3,2,1,0:T(8,128)S(1)} %get-tuple-element.12), channel_id=1, source_target_pairs={{0,8},{8,0},{16,24},{24,16},{32,40},{40,32},{48,56},{56,48},{64,72... | collective-permute-start | bytes 4718600 | tf_op jit(solution)/shard_map/ppermute | solution.py:232
  8.6 59.2 %copy-start.2 = (bf16[1536,128]{1,0:T(8,128)(2,1)S(1)}, bf16[1536,128]{1,0:T(8,128)(2,1)}, u32[]{:S(2)}) copy-start(bf16[1536,128]{1,0:T(8,128)(2,1)} %constant.9.clone.right) | copy-start | bytes 1179652
  8.6 59.2 %copy-start.3 = (f32[1,2,4096]{2,1,0:T(2,128)S(1)}, f32[1,2,4096]{2,1,0:T(2,128)}, u32[]{:S(2)}) copy-start(f32[1,2,4096]{2,1,0:T(2,128)} %momentum.1) | copy-start | bytes 98308
  8.6 59.2 %copy-start.5 = (bf16[64,192]{1,0:T(8,128)(2,1)S(1)}, bf16[64,192]{1,0:T(8,128)(2,1)}, u32[]{:S(2)}) copy-start(bf16[64,192]{1,0:T(8,128)(2,1)} %constant.8.clone.left) | copy-start | bytes 73732
  8.6 59.2 %copy-start.6 = (s32[2,2]{1,0:T(2,128)S(1)}, s32[2,2]{1,0:T(2,128)}, u32[]{:S(2)}) copy-start(s32[2,2]{1,0:T(2,128)} %corner.1) | copy-start | bytes 52
  8.6 20.6 %collective-permute-start.1 = (f32[12,64,128]{2,1,0:T(8,128)S(1)}, f32[12,64,128]{2,1,0:T(8,128)S(1)}, u32[]{:S(2)}, u32[]{:S(2)}) collective-permute-start(f32[12,64,128]{2,1,0:T(8,128)S(1)} %get-tuple-element.14), channel_id=1, source_target_pairs={{0,16},{8,184},{16,32},{24,8},{32,48},{40,24},{48,64},{56,40},{64,... | collective-permute-start | bytes 1179656 | tf_op jit(solution)/shard_map/ppermute | solution.py:235
  13.0 25.9 %collective-permute-start.2 = (f32[12,64,128]{2,1,0:T(8,128)S(1)}, f32[12,64,128]{2,1,0:T(8,128)S(1)}, u32[]{:S(2)}, u32[]{:S(2)}) collective-permute-start(f32[12,64,128]{2,1,0:T(8,128)S(1)} %get-tuple-element.15), channel_id=1, source_target_pairs={{0,176},{8,24},{16,0},{24,40},{32,16},{40,56},{48,32},{56,72},{64,... | collective-permute-start | bytes 1179656 | tf_op jit(solution)/shard_map/ppermute | solution.py:236
  25.3 15.2 %collective-permute-start.3 = (f32[12,64,128]{2,1,0:T(8,128)S(1)}, f32[12,64,128]{2,1,0:T(8,128)S(1)}, u32[]{:S(2)}, u32[]{:S(2)}) collective-permute-start(f32[12,64,128]{2,1,0:T(8,128)S(1)} %get-tuple-element.16), channel_id=1, source_target_pairs={{0,32},{8,168},{16,48},{24,184},{32,64},{40,8},{48,80},{56,24},{64... | collective-permute-start | bytes 1179656 | tf_op jit(solution)/shard_map/ppermute | solution.py:234
  40.5 39.3 %copy-start.1 = (bf16[384,512]{1,0:T(8,128)(2,1)S(1)}, bf16[384,512]{1,0:T(8,128)(2,1)}, u32[]{:S(2)}) copy-start(bf16[384,512]{1,0:T(8,128)(2,1)} %constant.11.clone.right_t) | copy-start | bytes 1179652
  40.5 39.3 %copy-start.4 = (bf16[64,192]{1,0:T(8,128)(2,1)S(1)}, bf16[64,192]{1,0:T(8,128)(2,1)}, u32[]{:S(2)}) copy-start(bf16[64,192]{1,0:T(8,128)(2,1)} %constant.10.clone.left_t) | copy-start | bytes 73732
